TPU v7x, 128 devices: a whole 4x4x4 slice. The times are simulated.
128 devices in a mesh: ctx: 16 (over x, y), chan: 8 (over z, core).
Axes of the slice: x: 4, y: 4, z: 4, core: 2. Of those that a mesh axis runs over, the one named last changes fastest.
Arguments:
- projections: bfloat16 [3, 256, 65536], P(None, 'chan', 'ctx'), may hold values from -6 to 6
- short_taps: float32 [3, 3, 256], P(None, None, 'chan'), may hold values from -1 to 1
- long_filter: bfloat16 [256, 65536], P('chan', 'ctx'), may hold values from -2 to 2
Outputs:
- gated: bfloat16 [256, 65536], P('chan', 'ctx')
All inputs are finite; a program needn't handle non-finite values.
Results may differ from a plain program's by a relative error of at most 0.014.
Values may be sent and summed in bfloat16 or wider, within the bound.
A program may use at most 64 MiB of HBM per device.

v0:
```python
import functools

import jax
import jax.numpy as jnp
import ml_dtypes
import numpy as np
from jax import lax
from jax.experimental import pallas as pl
from jax.experimental.pallas import tpu as pltpu
from jax.sharding import PartitionSpec as P

MESH = pl.DeviceIdType.MESH
LANES = 128
SIDE = 256
TOTAL = SIDE * SIDE


def tables():
    k = np.arange(SIDE, dtype=np.float64)

    def cis(a, b, length):
        angle = 2.0 * np.pi * np.fmod(a[:, None] * b[None, :], length) / length
        return np.cos(angle), np.sin(angle)

    cos, sin = cis(k + 0.25, k, SIDE)
    rows = np.concatenate([cos, -sin], axis=0)
    back_rows = np.concatenate([cos.T, -sin.T], axis=1) / TOTAL
    twist = np.stack(cis(k + 0.25, k, TOTAL))
    cos, sin = cis(k, k, SIDE)
    columns = np.block([[cos, -sin], [sin, cos]])
    back_columns = np.block([[cos, sin], [-sin, cos]])
    bf16 = ml_dtypes.bfloat16
    return (
        rows.astype(bf16),
        columns.astype(bf16),
        back_columns.astype(bf16),
        back_rows.astype(bf16),
        twist.astype(np.float32),
    )


def kernel(
    n,
    proj_hbm, filt_hbm, taps_ref, rows_hbm, cols_hbm, bcols_hbm, brows_hbm, twist_hbm,
    out_hbm,
    proj, filt, rows, cols, bcols, brows, twist, gate, stage,
    h_out, x_out, y_out, h_in, x_in, y_in, h_freq, back, out,
    load_sem, halo_send, halo_recv, h_send, h_recv, x_send, x_recv, y_send, y_recv, own_sem, out_sem,
):
    f32, bf16 = jnp.float32, jnp.bfloat16
    me = lax.axis_index("ctx")
    width = filt.shape[1]
    tiles = width // LANES
    half = filt.shape[0] // 2

    loads = [
        pltpu.make_async_copy(filt_hbm, filt, load_sem.at[0]),
        pltpu.make_async_copy(proj_hbm, proj.at[:, :, pl.ds(LANES, width)], load_sem.at[1]),
        pltpu.make_async_copy(rows_hbm, rows, load_sem.at[2]),
        pltpu.make_async_copy(twist_hbm, twist, load_sem.at[3]),
        pltpu.make_async_copy(cols_hbm, cols, load_sem.at[4]),
        pltpu.make_async_copy(bcols_hbm, bcols, load_sem.at[5]),
        pltpu.make_async_copy(brows_hbm, brows, load_sem.at[6]),
    ]
    for load in loads:
        load.start()

    barrier = pltpu.get_barrier_semaphore()

    def greet(step, carry):
        peer = lax.rem(me + step, n)
        pl.semaphore_signal(barrier, inc=1, device_id={"ctx": peer}, device_id_type=MESH)
        return carry

    lax.fori_loop(1, n, greet, 0)

    def block(ref, at):
        return ref.at[pl.ds(pl.multiple_of(at * 16, 16), 16)]

    def send_all(source, target, send_sem, recv_sem, own):
        def send(step, carry):
            peer = lax.rem(me + step, n)
            pltpu.make_async_remote_copy(
                src_ref=block(source, peer), dst_ref=block(target, me), send_sem=send_sem, recv_sem=recv_sem,
                device_id={"ctx": peer}, device_id_type=MESH,
            ).start()
            return carry

        lax.fori_loop(1, n, send, 0)
        pltpu.make_async_copy(block(source, me), block(target, me), own).start()

    def others(ref, send_sem, recv_sem):
        part = ref.at[pl.ds(0, 16 * (n - 1))]
        return pltpu.make_async_remote_copy(
            src_ref=part, dst_ref=part, send_sem=send_sem, recv_sem=recv_sem, device_id={"ctx": me}, device_id_type=MESH
        )

    def arrived(target, recv_sem, own):
        others(target, recv_sem, recv_sem).wait_recv()
        pltpu.make_async_copy(block(target, me), block(target, me), own).wait()

    def spread(value, group, tile_row, parity):
        stage[parity, pl.ds(group * 8 * 16 + tile_row, 8, stride=16), :] = value

    def gathered(target):
        target[:, 0:LANES] = stage[0].astype(bf16)
        target[:, LANES:SIDE] = stage[1].astype(bf16)

    loads[0].wait()

    def place_filter(j):
        def tile_pair(row, carry):
            for parity in range(2):
                at = pl.multiple_of((2 * row + parity) * LANES, LANES)
                value = filt[half * j : half * (j + 1), pl.ds(at, LANES)].astype(f32)
                for group in range(2):
                    spread(value[8 * group : 8 * group + 8], group, row, parity)
            return carry

        lax.fori_loop(0, tiles // 2, tile_pair, 0)
        gathered(h_out.at[j])

    place_filter(0)
    loads[1].wait()
    pl.semaphore_wait(barrier, n - 1)

    halo = pltpu.make_async_remote_copy(
        src_ref=proj.at[:, :, pl.ds(width, LANES)], dst_ref=proj.at[:, :, pl.ds(0, LANES)],
        send_sem=halo_send, recv_sem=halo_recv, device_id={"ctx": lax.rem(me + 1, n)}, device_id_type=MESH,
    )

    @pl.when(me < n - 1)
    def _():
        halo.start()

    @pl.when(me == 0)
    def _():
        proj[:, :, 0:LANES] = jnp.zeros((3, 2 * half, LANES), bf16)

    send_all(h_out.at[0], h_in.at[0], h_send.at[0], h_recv.at[0], own_sem.at[0])
    place_filter(1)
    send_all(h_out.at[1], h_in.at[1], h_send.at[1], h_recv.at[1], own_sem.at[1])

    diagonal = lax.broadcasted_iota(jnp.int32, (half, 2 * half), 0)
    along = lax.broadcasted_iota(jnp.int32, (half, 2 * half), 1)
    lane = lax.broadcasted_iota(jnp.int32, (half, LANES), 1)

    def tap(stream, lag, j):
        row = jnp.broadcast_to(taps_ref[stream, lag, :][None, :], (half, 2 * half))
        column = jnp.sum(jnp.where(along == diagonal + half * j, row, 0.0), axis=1, keepdims=True)
        return jnp.broadcast_to(column, (half, LANES))

    def tile_of(stream, at, j):
        start = pl.multiple_of(at * LANES, LANES)
        value = proj[stream, half * j : half * (j + 1), pl.ds(start, LANES)].astype(f32)
        return value, pltpu.roll(value, 1, 1), pltpu.roll(value, 2, 1)

    def short(taps, now, before):
        one = jnp.where(lane < 1, before[1], now[1])
        two = jnp.where(lane < 2, before[2], now[2])
        return taps[0] * now[0] + taps[1] * one + taps[2] * two

    def place_mixed(j):
        taps = [[tap(stream, lag, j) for lag in range(3)] for stream in (1, 2)]

        def one_tile(row, parity, now):
            before = [tile_of(stream, 2 * row + parity, j) for stream in (1, 2)]
            value = short(taps[0], now[0], before[0]) * short(taps[1], now[1], before[1])
            for group in range(2):
                spread(value[8 * group : 8 * group + 8], group, row, parity)
            return before

        def tile_pair(step, now):
            row = tiles // 2 - 1 - step
            return one_tile(row, 0, one_tile(row, 1, now))

        now = [tile_of(stream, tiles, j) for stream in (1, 2)]
        now = lax.fori_loop(0, tiles // 2 - 1, tile_pair, now)
        now = one_tile(0, 1, now)
        if j == 0:
            @pl.when(me > 0)
            def _():
                halo.wait_recv()
        one_tile(0, 0, now)
        gathered(x_out.at[j])
        send_all(x_out.at[j], x_in.at[j], x_send.at[j], x_recv.at[j], own_sem.at[2 + j])

    place_mixed(0)
    place_mixed(1)

    def place_gate(j):
        taps = [tap(0, lag, j) for lag in range(3)]

        def tile(at, before):
            now = tile_of(0, at + 1, j)
            gate[half * j : half * (j + 1), pl.ds(pl.multiple_of(at * LANES, LANES), LANES)] = short(taps, now, before)
            return now

        lax.fori_loop(0, tiles, tile, tile_of(0, 0, j))

    place_gate(0)
    place_gate(1)
    for load in loads[2:]:
        load.wait()

    def dot(a, b):
        return jnp.dot(a, b, preferred_element_type=f32)

    def forward(ref):
        part = dot(rows[...], ref[...])
        real, imag = part[:SIDE], part[SIDE:]
        cos, sin = twist[0], twist[1]
        turned = jnp.concatenate(
            [(real * cos + imag * sin).astype(bf16), (imag * cos - real * sin).astype(bf16)], axis=1
        )
        return dot(turned, cols[...])

    for j in range(2):
        arrived(h_in.at[j], h_recv.at[j], own_sem.at[j])
        h_freq[j] = forward(h_in.at[j])

    for j in range(2):
        arrived(x_in.at[j], x_recv.at[j], own_sem.at[2 + j])
        freq = forward(x_in.at[j])
        x_re, x_im = freq[:, :SIDE], freq[:, SIDE:]
        h_re, h_im = h_freq[j, :, :SIDE], h_freq[j, :, SIDE:]
        product = jnp.concatenate(
            [(x_re * h_re - x_im * h_im).astype(bf16), (x_re * h_im + x_im * h_re).astype(bf16)], axis=1
        )
        part = dot(product, bcols[...])
        real, imag = part[:, :SIDE], part[:, SIDE:]
        cos, sin = twist[0], twist[1]
        back[:SIDE] = (real * cos - imag * sin).astype(bf16)
        back[SIDE:] = (imag * cos + real * sin).astype(bf16)
        y_out[j] = dot(brows[...], back[...]).astype(bf16)
        send_all(y_out.at[j], y_in.at[j], y_send.at[j], y_recv.at[j], own_sem.at[4 + j])

    writes = []
    for j in range(2):
        arrived(y_in.at[j], y_recv.at[j], own_sem.at[4 + j])
        stage[0] = y_in[j, :, 0:LANES].astype(f32)
        stage[1] = y_in[j, :, LANES:SIDE].astype(f32)

        def tile_pair(row, carry):
            for parity in range(2):
                at = pl.multiple_of((2 * row + parity) * LANES, LANES)
                value = jnp.concatenate(
                    [stage[parity, pl.ds(group * 8 * 16 + row, 8, stride=16), :] for group in range(2)], axis=0
                )
                value = value * gate[half * j : half * (j + 1), pl.ds(at, LANES)]
                out[half * j : half * (j + 1), pl.ds(at, LANES)] = value.astype(bf16)
            return carry

        lax.fori_loop(0, tiles // 2, tile_pair, 0)
        channels = pl.ds(half * j, half)
        write = pltpu.make_async_copy(out.at[channels], out_hbm.at[channels], out_sem.at[j])
        write.start()
        writes.append(write)

    @pl.when(me < n - 1)
    def _():
        halo.wait_send()

    for j in range(2):
        others(h_out.at[j], h_send.at[j], h_send.at[j]).wait_send()
        others(x_out.at[j], x_send.at[j], x_send.at[j]).wait_send()
        others(y_out.at[j], y_send.at[j], y_send.at[j]).wait_send()
    for write in writes:
        write.wait()


def shards(n, projections, short_taps, long_filter):
    channels, width = long_filter.shape
    f32, bf16 = jnp.float32, jnp.bfloat16
    anywhere = pl.BlockSpec(memory_space=pl.ANY)
    square = pltpu.VMEM((2, SIDE, SIDE), bf16)
    pair = pltpu.SemaphoreType.DMA((2,))
    one = pltpu.SemaphoreType.DMA
    return pl.pallas_call(
        functools.partial(kernel, n),
        out_shape=jax.ShapeDtypeStruct((channels, width), bf16),
        in_specs=[anywhere, anywhere, pl.BlockSpec(memory_space=pltpu.VMEM)] + [anywhere] * 5,
        out_specs=anywhere,
        scratch_shapes=[
            pltpu.VMEM((3, channels, LANES + width), bf16),
            pltpu.VMEM((channels, width), bf16),
            pltpu.VMEM((2 * SIDE, SIDE), bf16),
            pltpu.VMEM((2 * SIDE, 2 * SIDE), bf16),
            pltpu.VMEM((2 * SIDE, 2 * SIDE), bf16),
            pltpu.VMEM((SIDE, 2 * SIDE), bf16),
            pltpu.VMEM((2, SIDE, SIDE), f32),
            pltpu.VMEM((channels, width), f32),
            pltpu.VMEM((2, SIDE, LANES), f32),
            square, square, square, square, square, square,
            pltpu.VMEM((2, SIDE, 2 * SIDE), f32),
            pltpu.VMEM((2 * SIDE, SIDE), bf16),
            pltpu.VMEM((channels, width), bf16),
            pltpu.SemaphoreType.DMA((7,)),
            one, one, pair, pair, pair, pair, pair, pair,
            pltpu.SemaphoreType.DMA((6,)),
            pair,
        ],
        compiler_params=pltpu.CompilerParams(
            collective_id=0, has_side_effects=True, vmem_limit_bytes=32 * 1024 * 1024
        ),
        name="long_convolution",
    )(projections, long_filter, short_taps, *(jnp.asarray(t) for t in tables()))


def solution(mesh):
    in_specs = (P(None, "chan", "ctx"), P(None, None, "chan"), P("chan", "ctx"))
    return jax.shard_map(
        functools.partial(shards, mesh.shape["ctx"]),
        mesh=mesh, in_specs=in_specs, out_specs=P("chan", "ctx"), check_vma=False,
    )
```

profile of v0, /device:TPU:0, one launch (start us, length us, event | category | flops | bytes accessed | tf_op | source)
XLA Modules:
  0.0 33.3 jit_solution(11502564784395051862)
XLA Ops:
  0.0 0.0 copy-start
  0.0 1.1 %copy-done = bf16[3,32,4096]{2,1,0:T(8,128)(2,1)S(1)} copy-done((bf16[3,32,4096]{2,1,0:T(8,128)(2,1)S(1)}, bf16[3,32,4096]{2,1,0:T(8,128)(2,1)}, u32[]{:S(2)}) %copy-start) | copy-done | bytes 786456
  1.1 0.0 copy-start.1
  1.1 1.0 %copy-done.1 = f32[2,256,256]{2,1,0:T(8,128)S(1)} copy-done((f32[2,256,256]{2,1,0:T(8,128)S(1)}, f32[2,256,256]{2,1,0:T(8,128)}, u32[]{:S(2)}) %copy-start.1) | copy-done | bytes 524312
  2.2 0.0 copy-start.2
  2.2 1.0 %copy-done.2 = bf16[512,512]{1,0:T(8,128)(2,1)S(1)} copy-done((bf16[512,512]{1,0:T(8,128)(2,1)S(1)}, bf16[512,512]{1,0:T(8,128)(2,1)}, u32[]{:S(2)}) %copy-start.2) | copy-done | bytes 524312
  3.2 0.0 copy-start.3
  3.2 1.0 %copy-done.3 = bf16[512,512]{1,0:T(8,128)(2,1)S(1)} copy-done((bf16[512,512]{1,0:T(8,128)(2,1)S(1)}, bf16[512,512]{1,0:T(8,128)(2,1)}, u32[]{:S(2)}) %copy-start.3) | copy-done | bytes 524312
  4.3 0.0 copy-start.4
  4.3 0.9 %copy-done.4 = bf16[32,4096]{1,0:T(8,128)(2,1)S(1)} copy-done((bf16[32,4096]{1,0:T(8,128)(2,1)S(1)}, bf16[32,4096]{1,0:T(8,128)(2,1)}, u32[]{:S(2)}) %copy-start.4) | copy-done | bytes 262168
  5.2 0.0 copy-start.5
  5.2 0.9 %copy-done.5 = bf16[256,512]{1,0:T(8,128)(2,1)S(1)} copy-done((bf16[256,512]{1,0:T(8,128)(2,1)S(1)}, bf16[256,512]{1,0:T(8,128)(2,1)}, u32[]{:S(2)}) %copy-start.5) | copy-done | bytes 262168
  6.2 0.0 copy-start.6
  6.2 0.9 %copy-done.6 = bf16[512,256]{1,0:T(8,128)(2,1)S(1)} copy-done((bf16[512,256]{1,0:T(8,128)(2,1)S(1)}, bf16[512,256]{1,0:T(8,128)(2,1)}, u32[]{:S(2)}) %copy-start.6) | copy-done | bytes 262168
  7.1 0.0 copy-start.7
  7.1 0.7 %copy-done.7 = f32[3,3,32]{2,1,0:T(4,128)S(1)} copy-done((f32[3,3,32]{2,1,0:T(4,128)S(1)}, f32[3,3,32]{2,1,0:T(4,128)}, u32[]{:S(2)}) %copy-start.7) | copy-done | bytes 1176
  7.8 24.8 %long_convolution.1 = bf16[32,4096]{1,0:T(8,128)(2,1)S(1)} custom-call(bf16[3,32,4096]{2,1,0:T(8,128)(2,1)S(1)} %copy-done, bf16[32,4096]{1,0:T(8,128)(2,1)S(1)} %copy-done.4, f32[3,3,32]{2,1,0:T(4,128)S(1)} %copy-done.7, bf16[512,256]{1,0:T(8,128)(2,1)S(1)} %copy-done.6, bf16[512,512]{1,0:T(8,128)(2,1)S(1)} %copy-done.3, bf16[512,512]{1,0:T(8,128)(2,1)S(1)} %copy-done.2, ...), custom_call_target="tpu_custom_call" | custom-call | tf_op jit(solution)/shard_map/long_convolution/pallas_call | solution.py:279
  32.6 0.7 %copy.10 = bf16[32,4096]{1,0:T(8,128)(2,1)} copy(bf16[32,4096]{1,0:T(8,128)(2,1)S(1)} %long_convolution.1) | data formatting | bytes 524288
Async XLA Ops:
  0.0 1.1 %copy-start = (bf16[3,32,4096]{2,1,0:T(8,128)(2,1)S(1)}, bf16[3,32,4096]{2,1,0:T(8,128)(2,1)}, u32[]{:S(2)}) copy-start(bf16[3,32,4096]{2,1,0:T(8,128)(2,1)} %proj_hbm.1) | copy-start | bytes 2359300
  1.1 1.0 %copy-start.1 = (f32[2,256,256]{2,1,0:T(8,128)S(1)}, f32[2,256,256]{2,1,0:T(8,128)}, u32[]{:S(2)}) copy-start(f32[2,256,256]{2,1,0:T(8,128)} %constant.14.clone.twist_hbm) | copy-start | bytes 1572868
  2.2 1.0 %copy-start.2 = (bf16[512,512]{1,0:T(8,128)(2,1)S(1)}, bf16[512,512]{1,0:T(8,128)(2,1)}, u32[]{:S(2)}) copy-start(bf16[512,512]{1,0:T(8,128)(2,1)} %constant.12.clone.bcols_hbm) | copy-start | bytes 1572868
  3.2 1.0 %copy-start.3 = (bf16[512,512]{1,0:T(8,128)(2,1)S(1)}, bf16[512,512]{1,0:T(8,128)(2,1)}, u32[]{:S(2)}) copy-start(bf16[512,512]{1,0:T(8,128)(2,1)} %constant.11.clone.cols_hbm) | copy-start | bytes 1572868
  4.3 0.9 %copy-start.4 = (bf16[32,4096]{1,0:T(8,128)(2,1)S(1)}, bf16[32,4096]{1,0:T(8,128)(2,1)}, u32[]{:S(2)}) copy-start(bf16[32,4096]{1,0:T(8,128)(2,1)} %filt_hbm.1) | copy-start | bytes 786436
  5.2 0.9 %copy-start.5 = (bf16[256,512]{1,0:T(8,128)(2,1)S(1)}, bf16[256,512]{1,0:T(8,128)(2,1)}, u32[]{:S(2)}) copy-start(bf16[256,512]{1,0:T(8,128)(2,1)} %constant.13.clone.brows_hbm) | copy-start | bytes 786436
  6.2 0.9 %copy-start.6 = (bf16[512,256]{1,0:T(8,128)(2,1)S(1)}, bf16[512,256]{1,0:T(8,128)(2,1)}, u32[]{:S(2)}) copy-start(bf16[512,256]{1,0:T(8,128)(2,1)} %constant.10.clone.rows_hbm) | copy-start | bytes 786436
  7.1 0.7 %copy-start.7 = (f32[3,3,32]{2,1,0:T(4,128)S(1)}, f32[3,3,32]{2,1,0:T(4,128)}, u32[]{:S(2)}) copy-start(f32[3,3,32]{2,1,0:T(4,128)} %taps_ref.1) | copy-start | bytes 3460
where the time goes:
time: 33.7 us; the launch traced here: 33.3 us
  Pallas kernels  24.8 us (74%)
  local copies, waits for them, and re-layouts  8.5 us (25%)
    pallas_call x1, Pallas kernels, shards(): pl.pallas_call(functools.partial(kernel, n), out_shape=jax.ShapeDtypeStru...  24.8 us
    unnamed x17, local copies, waits for them, and re-layouts  8.5 us

commit v1 on v0

--- a/solution.py
+++ b/solution.py
@@ -41,11 +41,11 @@
 
 def kernel(
     n,
-    proj_hbm, filt_hbm, taps_ref, rows_hbm, cols_hbm, bcols_hbm, brows_hbm, twist_hbm,
-    out_hbm,
-    proj, filt, rows, cols, bcols, brows, twist, gate, stage,
-    h_out, x_out, y_out, h_in, x_in, y_in, h_freq, back, out,
-    load_sem, halo_send, halo_recv, h_send, h_recv, x_send, x_recv, y_send, y_recv, own_sem, out_sem,
+    proj_hbm, filt_hbm, taps_hbm, rows_hbm, cols_hbm, bcols_hbm, brows_hbm, twist_hbm,
+    out,
+    proj, filt, taps_ref, rows, cols, bcols, brows, twist, gate, stage,
+    h_out, x_out, y_out, h_in, x_in, y_in, h_freq, back,
+    load_sem, halo_send, halo_recv, h_send, h_recv, x_send, x_recv, y_send, y_recv, own_sem,
 ):
     f32, bf16 = jnp.float32, jnp.bfloat16
     me = lax.axis_index("ctx")
@@ -56,11 +56,12 @@
     loads = [
         pltpu.make_async_copy(filt_hbm, filt, load_sem.at[0]),
         pltpu.make_async_copy(proj_hbm, proj.at[:, :, pl.ds(LANES, width)], load_sem.at[1]),
-        pltpu.make_async_copy(rows_hbm, rows, load_sem.at[2]),
-        pltpu.make_async_copy(twist_hbm, twist, load_sem.at[3]),
-        pltpu.make_async_copy(cols_hbm, cols, load_sem.at[4]),
-        pltpu.make_async_copy(bcols_hbm, bcols, load_sem.at[5]),
-        pltpu.make_async_copy(brows_hbm, brows, load_sem.at[6]),
+        pltpu.make_async_copy(taps_hbm, taps_ref, load_sem.at[2]),
+        pltpu.make_async_copy(rows_hbm, rows, load_sem.at[3]),
+        pltpu.make_async_copy(twist_hbm, twist, load_sem.at[4]),
+        pltpu.make_async_copy(cols_hbm, cols, load_sem.at[5]),
+        pltpu.make_async_copy(bcols_hbm, bcols, load_sem.at[6]),
+        pltpu.make_async_copy(brows_hbm, brows, load_sem.at[7]),
     ]
     for load in loads:
         load.start()
@@ -122,6 +123,7 @@
 
     place_filter(0)
     loads[1].wait()
+    loads[2].wait()
     pl.semaphore_wait(barrier, n - 1)
 
     halo = pltpu.make_async_remote_copy(
@@ -200,7 +202,7 @@
 
     place_gate(0)
     place_gate(1)
-    for load in loads[2:]:
+    for load in loads[3:]:
         load.wait()
 
     def dot(a, b):
@@ -235,7 +237,6 @@
         y_out[j] = dot(brows[...], back[...]).astype(bf16)
         send_all(y_out.at[j], y_in.at[j], y_send.at[j], y_recv.at[j], own_sem.at[4 + j])
 
-    writes = []
     for j in range(2):
         arrived(y_in.at[j], y_recv.at[j], own_sem.at[4 + j])
         stage[0] = y_in[j, :, 0:LANES].astype(f32)
@@ -252,10 +253,6 @@
             return carry
 
         lax.fori_loop(0, tiles // 2, tile_pair, 0)
-        channels = pl.ds(half * j, half)
-        write = pltpu.make_async_copy(out.at[channels], out_hbm.at[channels], out_sem.at[j])
-        write.start()
-        writes.append(write)
 
     @pl.when(me < n - 1)
     def _():
@@ -265,25 +262,26 @@
         others(h_out.at[j], h_send.at[j], h_send.at[j]).wait_send()
         others(x_out.at[j], x_send.at[j], x_send.at[j]).wait_send()
         others(y_out.at[j], y_send.at[j], y_send.at[j]).wait_send()
-    for write in writes:
-        write.wait()
 
 
 def shards(n, projections, short_taps, long_filter):
     channels, width = long_filter.shape
     f32, bf16 = jnp.float32, jnp.bfloat16
-    anywhere = pl.BlockSpec(memory_space=pl.ANY)
+    outside = pl.BlockSpec(memory_space=pltpu.HBM)
+    inside = pl.BlockSpec(memory_space=pltpu.VMEM)
     square = pltpu.VMEM((2, SIDE, SIDE), bf16)
     pair = pltpu.SemaphoreType.DMA((2,))
     one = pltpu.SemaphoreType.DMA
+    operands = [projections, long_filter, short_taps, *(jnp.asarray(t) for t in tables())]
     return pl.pallas_call(
         functools.partial(kernel, n),
         out_shape=jax.ShapeDtypeStruct((channels, width), bf16),
-        in_specs=[anywhere, anywhere, pl.BlockSpec(memory_space=pltpu.VMEM)] + [anywhere] * 5,
-        out_specs=anywhere,
+        in_specs=[outside] * 8,
+        out_specs=inside,
         scratch_shapes=[
             pltpu.VMEM((3, channels, LANES + width), bf16),
             pltpu.VMEM((channels, width), bf16),
+            pltpu.VMEM((3, 3, channels), f32),
             pltpu.VMEM((2 * SIDE, SIDE), bf16),
             pltpu.VMEM((2 * SIDE, 2 * SIDE), bf16),
             pltpu.VMEM((2 * SIDE, 2 * SIDE), bf16),
@@ -294,17 +292,15 @@
             square, square, square, square, square, square,
             pltpu.VMEM((2, SIDE, 2 * SIDE), f32),
             pltpu.VMEM((2 * SIDE, SIDE), bf16),
-            pltpu.VMEM((channels, width), bf16),
-            pltpu.SemaphoreType.DMA((7,)),
+            pltpu.SemaphoreType.DMA((8,)),
             one, one, pair, pair, pair, pair, pair, pair,
             pltpu.SemaphoreType.DMA((6,)),
-            pair,
         ],
         compiler_params=pltpu.CompilerParams(
             collective_id=0, has_side_effects=True, vmem_limit_bytes=32 * 1024 * 1024
         ),
         name="long_convolution",
-    )(projections, long_filter, short_taps, *(jnp.asarray(t) for t in tables()))
+    )(*(pltpu.with_memory_space_constraint(x, pltpu.HBM) for x in operands))
 
 
 def solution(mesh):

time: 33.7 us -> 25.2 us (0.75)
  local copies, waits for them, and re-layouts: 8.5 us -> 0.71 us
  Pallas kernels: 24.8 us -> 24.4 us
    unnamed x17 -> x1, local copies, waits for them, and re-layouts: 8.5 us -> 0.71 us
    pallas_call x1, Pallas kernels: 24.8 us -> 24.4 us  [shards(): pl.pallas_call(functools.partial(kernel, n), out_shape=jax.ShapeDtypeStru...]
where the time goes in v1:
time: 25.2 us; the launch traced here: 25.1 us
  Pallas kernels  24.4 us (97%)
  local copies, waits for them, and re-layouts  0.71 us (3%)
    pallas_call x1, Pallas kernels, shards(): pl.pallas_call(functools.partial(kernel, n), out_shape=jax.ShapeDtypeStru...  24.4 us
    unnamed x1, local copies, waits for them, and re-layouts  0.71 us

profile of v1, /device:TPU:0, one launch (start us, length us, event | category | flops | bytes accessed | tf_op | source)
XLA Modules:
  0.0 25.1 jit_solution(8816045953919376678)
XLA Ops:
  0.0 24.4 %long_convolution.1 = bf16[32,4096]{1,0:T(8,128)(2,1)S(1)} custom-call(bf16[3,32,4096]{2,1,0:T(8,128)(2,1)} %proj_hbm.1, bf16[32,4096]{1,0:T(8,128)(2,1)} %filt_hbm.1, f32[3,3,32]{2,1,0:T(4,128)} %taps_hbm.1, bf16[512,256]{1,0:T(8,128)(2,1)} %constant.10.clone.rows_hbm, bf16[512,512]{1,0:T(8,128)(2,1)} %constant.11.clone.cols_hbm, ...), custom_call_target="tpu_custom_call" | custom-call | tf_op jit(solution)/shard_map/long_convolution/pallas_call | solution.py:276
  24.4 0.7 %copy.10 = bf16[32,4096]{1,0:T(8,128)(2,1)} copy(bf16[32,4096]{1,0:T(8,128)(2,1)S(1)} %long_convolution.1) | data formatting | bytes 524288

commit v2 on v1

v2 whole, which is shorter than its diff:
```python
import functools
import math

import jax
import jax.numpy as jnp
import ml_dtypes
import numpy as np
from jax import lax
from jax.experimental import pallas as pl
from jax.experimental.pallas import tpu as pltpu
from jax.sharding import PartitionSpec as P

MESH = pl.DeviceIdType.MESH
LANES = 128
SIDE = 256
TOTAL = SIDE * SIDE


def tables():
    k = np.arange(SIDE, dtype=np.float64)

    def cis(a, b, length):
        angle = 2.0 * np.pi * np.fmod(a[:, None] * b[None, :], length) / length
        return np.cos(angle), np.sin(angle)

    cos, sin = cis(k + 0.25, k, SIDE)
    rows = np.concatenate([cos, -sin], axis=0)
    back_rows = np.concatenate([cos.T, -sin.T], axis=1) / TOTAL
    twist = np.stack(cis(k + 0.25, k, TOTAL))
    cos, sin = cis(k, k, SIDE)
    columns = np.block([[cos, -sin], [sin, cos]])
    back_columns = np.block([[cos, sin], [-sin, cos]])
    bf16 = ml_dtypes.bfloat16
    return (
        rows.astype(bf16),
        columns.astype(bf16),
        back_columns.astype(bf16),
        back_rows.astype(bf16),
        twist.astype(np.float32),
    )


def peers_of(me, n):
    side = math.isqrt(n)

    def hops(step):
        return sum(min(s, side - s) for s in step)

    steps = [(a, b) for a in range(side) for b in range(side) if a or b]
    row, column = me // side, lax.rem(me, side)
    return [
        lax.rem(row + a, side) * side + lax.rem(column + b, side)
        for a, b in sorted(steps, key=hops, reverse=True)
    ]


def kernel(
    n,
    proj_hbm, filt_hbm, taps_hbm, rows_hbm, cols_hbm, bcols_hbm, brows_hbm, twist_hbm,
    out,
    proj, filt, taps_ref, rows, cols, bcols, brows, twist, gate, stage, q_halo, head,
    h_out, x_out, y_out, h_in, x_in, y_in, e_out, e_in, h_freq, back,
    load_sem, halo_send, halo_recv, h_send, h_recv, x_send, x_recv, y_send, y_recv, e_send, e_recv, own_sem,
):
    f32, bf16 = jnp.float32, jnp.bfloat16
    me = lax.axis_index("ctx")
    peers = peers_of(me, n)
    width = filt.shape[1]
    tiles = width // LANES
    half = filt.shape[0] // 2

    barrier = pltpu.get_barrier_semaphore()
    for peer in peers:
        pl.semaphore_signal(barrier, inc=1, device_id={"ctx": peer}, device_id_type=MESH)
    loads = [
        pltpu.make_async_copy(source, target, load_sem.at[at])
        for at, (source, target) in enumerate([
            (filt_hbm, filt), (taps_hbm, taps_ref), (proj_hbm.at[1], proj.at[1]), (proj_hbm.at[2], proj.at[2]),
            (proj_hbm.at[0], proj.at[0]), (rows_hbm, rows), (twist_hbm, twist), (cols_hbm, cols),
            (bcols_hbm, bcols), (brows_hbm, brows),
        ])
    ]
    for load in loads:
        load.start()

    def block(ref, at):
        return ref.at[pl.ds(pl.multiple_of(at * 16, 16), 16)]

    def remote(source, target, send_sem, recv_sem, peer):
        return pltpu.make_async_remote_copy(
            src_ref=source, dst_ref=target, send_sem=send_sem, recv_sem=recv_sem,
            device_id={"ctx": peer}, device_id_type=MESH,
        )

    def send_all(source, target, send_sem, recv_sem, own, part=block):
        for peer in peers:
            remote(part(source, peer), part(target, me), send_sem, recv_sem, peer).start()
        pltpu.make_async_copy(part(source, me), part(target, me), own).start()

    def others(ref, send_sem, recv_sem):
        size = ref.shape[0] // n * (n - 1)
        return remote(ref.at[pl.ds(0, size)], ref.at[pl.ds(0, size)], send_sem, recv_sem, me)

    def arrived(target, recv_sem, own, part=block):
        others(target, recv_sem, recv_sem).wait_recv()
        pltpu.make_async_copy(part(target, me), part(target, me), own).wait()

    def spread(value, group, tile_row, parity):
        stage[parity, pl.ds(group * 8 * 16 + tile_row, 8, stride=16), :] = value

    def gathered(target):
        target[:, 0:LANES] = stage[0].astype(bf16)
        target[:, LANES:SIDE] = stage[1].astype(bf16)

    def place_filter(j):
        def tile_pair(row, carry):
            for parity in range(2):
                at = pl.multiple_of((2 * row + parity) * LANES, LANES)
                value = filt[half * j : half * (j + 1), pl.ds(at, LANES)].astype(f32)
                for group in range(2):
                    spread(value[8 * group : 8 * group + 8], group, row, parity)
            return carry

        lax.fori_loop(0, tiles // 2, tile_pair, 0, unroll=True)
        gathered(h_out.at[j])

    diagonal = lax.broadcasted_iota(jnp.int32, (half, 2 * half), 0)
    along = lax.broadcasted_iota(jnp.int32, (half, 2 * half), 1)
    lane = lax.broadcasted_iota(jnp.int32, (half, LANES), 1)
    lag_range, zero = range(3), jnp.zeros((half, LANES), f32)

    def tap(stream, lag, j):
        row = jnp.broadcast_to(taps_ref[stream, lag, :][None, :], (half, 2 * half))
        column = jnp.sum(jnp.where(along == diagonal + half * j, row, 0.0), axis=1, keepdims=True)
        return jnp.broadcast_to(column, (half, LANES))

    def own_tap(stream, lag, j):
        row = jnp.broadcast_to(taps_ref[stream, lag, :][None, :], (half, 2 * half))
        column = jnp.sum(jnp.where(along == me + half * j, row, 0.0), axis=1, keepdims=True)
        return jnp.broadcast_to(column, (half, LANES))

    def rolled(value):
        return value, pltpu.roll(value, 1, 1), pltpu.roll(value, 2, 1)

    def tile_of(stream, at, j):
        start = pl.multiple_of(at * LANES, LANES)
        return rolled(proj[stream, half * j : half * (j + 1), pl.ds(start, LANES)].astype(f32))

    def short(taps, now, before):
        one = jnp.where(lane < 1, before[1], now[1])
        two = jnp.where(lane < 2, before[2], now[2])
        return taps[0] * now[0] + taps[1] * one + taps[2] * two

    def place_mixed(j):
        taps = [[tap(stream, lag, j) for lag in lag_range] for stream in (1, 2)]

        def one_tile(row, parity, now, before):
            value = short(taps[0], now[0], before[0]) * short(taps[1], now[1], before[1])
            for group in range(2):
                spread(value[8 * group : 8 * group + 8], group, row, parity)

        def tile_pair(row, before):
            for parity in range(2):
                now = [tile_of(stream, 2 * row + parity, j) for stream in (1, 2)]
                one_tile(row, parity, now, before)
                before = now
            return before

        lax.fori_loop(0, tiles // 2, tile_pair, [(zero, zero, zero)] * 2, unroll=True)
        gathered(x_out.at[j])

    def place_edges():
        edges = zero
        for g in range(4):
            channels = slice(half * (g // 2), half * (g // 2) + half)
            first = proj[1 + g % 2, channels, 0:LANES].astype(f32)
            last = proj[1 + g % 2, channels, width - LANES : width].astype(f32)
            edges = jnp.where((lane >= 32 * g) & (lane < 32 * g + 16), pltpu.roll(first, 32 * g, 1) if g else first, edges)
            edges = jnp.where(
                (lane >= 32 * g + 16) & (lane < 32 * g + 32), pltpu.roll(last, 32 * (g + 1), 1) if g < 3 else last, edges
            )
        e_out[...] = edges[:, None, :]

    def place_heads():
        edges = e_in[...].reshape(n, LANES)
        earlier = jnp.where(lax.broadcasted_iota(jnp.int32, (n, LANES), 0) < 1, 0.0, pltpu.roll(edges, 1, 0))
        for j in range(2):
            product = None
            for stream in (1, 2):
                g = 2 * j + stream - 1
                now = pltpu.roll(edges, LANES - 32 * g, 1) if g else edges
                one = jnp.where(lane < 1, pltpu.roll(earlier, (2 * LANES - 32 * g - 31) % LANES, 1), pltpu.roll(now, 1, 1))
                two = pltpu.roll(earlier, (2 * LANES - 32 * g - 30) % LANES, 1)
                taps = [own_tap(stream, lag, j) for lag in lag_range]
                value = taps[0] * now + taps[1] * one + taps[2] * two
                product = value if product is None else product * value
            for group in range(2):
                head[j, pl.ds(group * 8 * 16, 8, stride=16), :] = product[8 * group : 8 * group + 8]

    def mixed_of(j):
        at_row = lax.broadcasted_iota(jnp.int32, (SIDE, LANES), 0)
        at_lane = lax.broadcasted_iota(jnp.int32, (SIDE, LANES), 1)
        is_head = (lax.rem(at_row, 16) == 0) & (at_lane < 2)
        even = jnp.where(is_head, head[j], x_in[j, :, 0:LANES].astype(f32)).astype(bf16)
        return jnp.concatenate([even, x_in[j, :, LANES:SIDE]], axis=1)

    def place_gate(j):
        taps = [tap(0, lag, j) for lag in lag_range]

        def tile(at, before):
            now = tile_of(0, at, j)
            gate[half * j : half * (j + 1), pl.ds(pl.multiple_of(at * LANES, LANES), LANES)] = short(taps, now, before)
            return now

        before = rolled(jnp.where(me > 0, q_halo[half * j : half * (j + 1), :].astype(f32), 0.0))
        lax.fori_loop(0, tiles, tile, before, unroll=True)

    def dot(a, b):
        return jnp.dot(a, b, preferred_element_type=f32)

    def forward(value):
        part = dot(rows[...], value)
        real, imag = part[:SIDE], part[SIDE:]
        cos, sin = twist[0], twist[1]
        turned = jnp.concatenate(
            [(real * cos + imag * sin).astype(bf16), (imag * cos - real * sin).astype(bf16)], axis=1
        )
        return dot(turned, cols[...])

    def whole(ref, at):
        return ref.at[pl.ds(at, 1)]

    loads[0].wait()
    place_filter(0)
    place_filter(1)
    for load in loads[1:4]:
        load.wait()
    place_edges()
    pl.semaphore_wait(barrier, n - 1)
    send_all(h_out.at[0], h_in.at[0], h_send.at[0], h_recv.at[0], own_sem.at[0])
    send_all(e_out, e_in, e_send, e_recv, own_sem.at[6], part=whole)
    place_mixed(0)
    send_all(x_out.at[0], x_in.at[0], x_send.at[0], x_recv.at[0], own_sem.at[2])
    send_all(h_out.at[1], h_in.at[1], h_send.at[1], h_recv.at[1], own_sem.at[1])
    place_mixed(1)
    send_all(x_out.at[1], x_in.at[1], x_send.at[1], x_recv.at[1], own_sem.at[3])
    loads[4].wait()
    last = proj.at[0, :, pl.ds(width - LANES, LANES)]
    halo = remote(last, q_halo, halo_send, halo_recv, lax.rem(me + 1, n))
    halo.start()
    for load in loads[5:]:
        load.wait()

    for j in range(2):
        arrived(h_in.at[j], h_recv.at[j], own_sem.at[j])
        h_freq[...] = forward(h_in[j])
        if j == 0:
            arrived(e_in, e_recv, own_sem.at[6], part=whole)
            place_heads()
        arrived(x_in.at[j], x_recv.at[j], own_sem.at[2 + j])
        freq = forward(mixed_of(j))
        x_re, x_im = freq[:, :SIDE], freq[:, SIDE:]
        h_re, h_im = h_freq[:, :SIDE], h_freq[:, SIDE:]
        product = jnp.concatenate(
            [(x_re * h_re - x_im * h_im).astype(bf16), (x_re * h_im + x_im * h_re).astype(bf16)], axis=1
        )
        part = dot(product, bcols[...])
        real, imag = part[:, :SIDE], part[:, SIDE:]
        cos, sin = twist[0], twist[1]
        back[:SIDE] = (real * cos - imag * sin).astype(bf16)
        back[SIDE:] = (imag * cos + real * sin).astype(bf16)
        y_out[j] = dot(brows[...], back[...]).astype(bf16)
        send_all(y_out.at[j], y_in.at[j], y_send.at[j], y_recv.at[j], own_sem.at[4 + j])

    halo.wait_recv()
    place_gate(0)
    place_gate(1)

    for j in range(2):
        arrived(y_in.at[j], y_recv.at[j], own_sem.at[4 + j])
        stage[0] = y_in[j, :, 0:LANES].astype(f32)
        stage[1] = y_in[j, :, LANES:SIDE].astype(f32)

        def tile_pair(row, carry):
            for parity in range(2):
                at = pl.multiple_of((2 * row + parity) * LANES, LANES)
                value = jnp.concatenate(
                    [stage[parity, pl.ds(group * 8 * 16 + row, 8, stride=16), :] for group in range(2)], axis=0
                )
                value = value * gate[half * j : half * (j + 1), pl.ds(at, LANES)]
                out[half * j : half * (j + 1), pl.ds(at, LANES)] = value.astype(bf16)
            return carry

        lax.fori_loop(0, tiles // 2, tile_pair, 0, unroll=True)

    halo.wait_send()
    others(e_out, e_send, e_send).wait_send()
    for j in range(2):
        others(h_out.at[j], h_send.at[j], h_send.at[j]).wait_send()
        others(x_out.at[j], x_send.at[j], x_send.at[j]).wait_send()
        others(y_out.at[j], y_send.at[j], y_send.at[j]).wait_send()


def shards(n, projections, short_taps, long_filter):
    channels, width = long_filter.shape
    f32, bf16 = jnp.float32, jnp.bfloat16
    outside = pl.BlockSpec(memory_space=pltpu.HBM)
    inside = pl.BlockSpec(memory_space=pltpu.VMEM)
    square = pltpu.VMEM((2, SIDE, SIDE), bf16)
    edges = pltpu.VMEM((n, 1, LANES), f32)
    pair = pltpu.SemaphoreType.DMA((2,))
    one = pltpu.SemaphoreType.DMA
    operands = [projections, long_filter, short_taps, *(jnp.asarray(t) for t in tables())]
    return pl.pallas_call(
        functools.partial(kernel, n),
        out_shape=jax.ShapeDtypeStruct((channels, width), bf16),
        in_specs=[outside] * 8,
        out_specs=inside,
        scratch_shapes=[
            pltpu.VMEM((3, channels, width), bf16),
            pltpu.VMEM((channels, width), bf16),
            pltpu.VMEM((3, 3, channels), f32),
            pltpu.VMEM((2 * SIDE, SIDE), bf16),
            pltpu.VMEM((2 * SIDE, 2 * SIDE), bf16),
            pltpu.VMEM((2 * SIDE, 2 * SIDE), bf16),
            pltpu.VMEM((SIDE, 2 * SIDE), bf16),
            pltpu.VMEM((2, SIDE, SIDE), f32),
            pltpu.VMEM((channels, width), f32),
            pltpu.VMEM((2, SIDE, LANES), f32),
            pltpu.VMEM((channels, LANES), bf16),
            pltpu.VMEM((2, SIDE, LANES), f32),
            square, square, square, square, square, square,
            edges, edges,
            pltpu.VMEM((SIDE, 2 * SIDE), f32),
            pltpu.VMEM((2 * SIDE, SIDE), bf16),
            pltpu.SemaphoreType.DMA((10,)),
            one, one, pair, pair, pair, pair, pair, pair, one, one,
            pltpu.SemaphoreType.DMA((7,)),
        ],
        compiler_params=pltpu.CompilerParams(
            collective_id=0, has_side_effects=True, vmem_limit_bytes=32 * 1024 * 1024
        ),
        name="long_convolution",
    )(*(pltpu.with_memory_space_constraint(x, pltpu.HBM) for x in operands))


def solution(mesh):
    in_specs = (P(None, "chan", "ctx"), P(None, None, "chan"), P("chan", "ctx"))
    return jax.shard_map(
        functools.partial(shards, mesh.shape["ctx"]),
        mesh=mesh, in_specs=in_specs, out_specs=P("chan", "ctx"), check_vma=False,
    )
```

time: 25.2 us -> 21.6 us (0.86)
  Pallas kernels: 24.4 us -> 20.8 us
    pallas_call x1, Pallas kernels: 24.4 us -> 20.8 us  [shards(): pl.pallas_call(functools.partial(kernel, n), out_shape=jax.ShapeDtypeStru...]
where the time goes in v2:
time: 21.6 us; the launch traced here: 21.5 us
  Pallas kernels  20.8 us (96%)
  local copies, waits for them, and re-layouts  0.71 us (3%)
    pallas_call x1, Pallas kernels, shards(): pl.pallas_call(functools.partial(kernel, n), out_shape=jax.ShapeDtypeStru...  20.8 us
    unnamed x1, local copies, waits for them, and re-layouts  0.71 us

profile of v2, /device:TPU:0, one launch (start us, length us, event | category | flops | bytes accessed | tf_op | source)
XLA Modules:
  0.0 21.5 jit_solution(12300119933266588537)
XLA Ops:
  0.0 20.8 %long_convolution.1 = bf16[32,4096]{1,0:T(8,128)(2,1)S(1)} custom-call(bf16[3,32,4096]{2,1,0:T(8,128)(2,1)} %proj_hbm.1, bf16[32,4096]{1,0:T(8,128)(2,1)} %filt_hbm.1, f32[3,3,32]{2,1,0:T(4,128)} %taps_hbm.1, bf16[512,256]{1,0:T(8,128)(2,1)} %constant.10.clone.rows_hbm, bf16[512,512]{1,0:T(8,128)(2,1)} %constant.11.clone.cols_hbm, ...), custom_call_target="tpu_custom_call" | custom-call | tf_op jit(solution)/shard_map/long_convolution/pallas_call | solution.py:314
  20.8 0.7 %copy.10 = bf16[32,4096]{1,0:T(8,128)(2,1)} copy(bf16[32,4096]{1,0:T(8,128)(2,1)S(1)} %long_convolution.1) | data formatting | bytes 524288

commit v3 on v2

--- a/solution.py
+++ b/solution.py
@@ -40,18 +40,10 @@
     )
 
 
-def peers_of(me, n):
+def steps_of(n):
     side = math.isqrt(n)
-
-    def hops(step):
-        return sum(min(s, side - s) for s in step)
-
     steps = [(a, b) for a in range(side) for b in range(side) if a or b]
-    row, column = me // side, lax.rem(me, side)
-    return [
-        lax.rem(row + a, side) * side + lax.rem(column + b, side)
-        for a, b in sorted(steps, key=hops, reverse=True)
-    ]
+    return sorted(steps, key=lambda step: -sum(min(s, side - s) for s in step))
 
 
 def kernel(
@@ -59,19 +51,26 @@
     proj_hbm, filt_hbm, taps_hbm, rows_hbm, cols_hbm, bcols_hbm, brows_hbm, twist_hbm,
     out,
     proj, filt, taps_ref, rows, cols, bcols, brows, twist, gate, stage, q_halo, head,
-    h_out, x_out, y_out, h_in, x_in, y_in, e_out, e_in, h_freq, back,
-    load_sem, halo_send, halo_recv, h_send, h_recv, x_send, x_recv, y_send, y_recv, e_send, e_recv, own_sem,
+    h_out, x_out, y_out, h_in, x_in, y_in, e_out, e_in, h_freq,
+    load_sem, halo_send, halo_recv, h_send, h_recv, x_send, x_recv, y_send, y_recv, e_send, e_recv, own_sem, column_in,
 ):
     f32, bf16 = jnp.float32, jnp.bfloat16
     me = lax.axis_index("ctx")
-    peers = peers_of(me, n)
+    side = math.isqrt(n)
+    my_row, my_column = me // side, lax.rem(me, side)
+
+    def device(step):
+        return lax.rem(my_row + step[0], side) * side + lax.rem(my_column + step[1], side)
+
+    steps = steps_of(n)
+    mates = [step for step in steps if not (step[0] and step[1])]
     width = filt.shape[1]
     tiles = width // LANES
     half = filt.shape[0] // 2
 
     barrier = pltpu.get_barrier_semaphore()
-    for peer in peers:
-        pl.semaphore_signal(barrier, inc=1, device_id={"ctx": peer}, device_id_type=MESH)
+    for step in mates:
+        pl.semaphore_signal(barrier, inc=1, device_id={"ctx": device(step)}, device_id_type=MESH)
     loads = [
         pltpu.make_async_copy(source, target, load_sem.at[at])
         for at, (source, target) in enumerate([
@@ -84,7 +83,7 @@
         load.start()
 
     def block(ref, at):
-        return ref.at[pl.ds(pl.multiple_of(at * 16, 16), 16)]
+        return ref.at[pl.ds(at, 1)]
 
     def remote(source, target, send_sem, recv_sem, peer):
         return pltpu.make_async_remote_copy(
@@ -92,9 +91,12 @@
             device_id={"ctx": peer}, device_id_type=MESH,
         )
 
-    def send_all(source, target, send_sem, recv_sem, own, part=block):
-        for peer in peers:
+    def send(source, target, send_sem, recv_sem, chosen, part=block):
+        for step in chosen:
+            peer = device(step)
             remote(part(source, peer), part(target, me), send_sem, recv_sem, peer).start()
+
+    def keep(source, target, own, part=block):
         pltpu.make_async_copy(part(source, me), part(target, me), own).start()
 
     def others(ref, send_sem, recv_sem):
@@ -109,8 +111,8 @@
         stage[parity, pl.ds(group * 8 * 16 + tile_row, 8, stride=16), :] = value
 
     def gathered(target):
-        target[:, 0:LANES] = stage[0].astype(bf16)
-        target[:, LANES:SIDE] = stage[1].astype(bf16)
+        for parity in range(2):
+            target[:, :, LANES * parity : LANES * (parity + 1)] = stage[parity].astype(bf16).reshape(n, 16, LANES)
 
     def place_filter(j):
         def tile_pair(row, carry):
@@ -201,8 +203,9 @@
         at_row = lax.broadcasted_iota(jnp.int32, (SIDE, LANES), 0)
         at_lane = lax.broadcasted_iota(jnp.int32, (SIDE, LANES), 1)
         is_head = (lax.rem(at_row, 16) == 0) & (at_lane < 2)
-        even = jnp.where(is_head, head[j], x_in[j, :, 0:LANES].astype(f32)).astype(bf16)
-        return jnp.concatenate([even, x_in[j, :, LANES:SIDE]], axis=1)
+        value = x_in[j].reshape(SIDE, SIDE)
+        even = jnp.where(is_head, head[j], value[:, 0:LANES].astype(f32)).astype(bf16)
+        return jnp.concatenate([even, value[:, LANES:SIDE]], axis=1)
 
     def place_gate(j):
         taps = [tap(0, lag, j) for lag in lag_range]
@@ -218,17 +221,33 @@
     def dot(a, b):
         return jnp.dot(a, b, preferred_element_type=f32)
 
-    def forward(value):
-        part = dot(rows[...], value)
-        real, imag = part[:SIDE], part[SIDE:]
+    def forward(values):
+        part = dot(rows[...], jnp.concatenate(values, axis=1))
+        cos, sin = twist[0], twist[1]
+        turned = []
+        for at in range(len(values)):
+            columns = slice(SIDE * at, SIDE * (at + 1))
+            real, imag = part[:SIDE, columns], part[SIDE:, columns]
+            turned.append(
+                jnp.concatenate([(real * cos + imag * sin).astype(bf16), (imag * cos - real * sin).astype(bf16)], axis=1)
+            )
+        return dot(jnp.concatenate(turned, axis=0), cols[...])
+
+    def convolved(x, h):
+        x_re, x_im, h_re, h_im = x[:, :SIDE], x[:, SIDE:], h[:, :SIDE], h[:, SIDE:]
+        product = jnp.concatenate(
+            [(x_re * h_re - x_im * h_im).astype(bf16), (x_re * h_im + x_im * h_re).astype(bf16)], axis=1
+        )
+        part = dot(product, bcols[...])
+        real, imag = part[:, :SIDE], part[:, SIDE:]
         cos, sin = twist[0], twist[1]
         turned = jnp.concatenate(
-            [(real * cos + imag * sin).astype(bf16), (imag * cos - real * sin).astype(bf16)], axis=1
+            [(real * cos - imag * sin).astype(bf16), (imag * cos + real * sin).astype(bf16)], axis=0
         )
-        return dot(turned, cols[...])
-
-    def whole(ref, at):
-        return ref.at[pl.ds(at, 1)]
+        return dot(brows[...], turned).astype(bf16).reshape(n, 16, SIDE)
+
+    def filter_of(j):
+        return h_in[j].reshape(SIDE, SIDE)
 
     loads[0].wait()
     place_filter(0)
@@ -236,14 +255,32 @@
     for load in loads[1:4]:
         load.wait()
     place_edges()
-    pl.semaphore_wait(barrier, n - 1)
-    send_all(h_out.at[0], h_in.at[0], h_send.at[0], h_recv.at[0], own_sem.at[0])
-    send_all(e_out, e_in, e_send, e_recv, own_sem.at[6], part=whole)
+    pl.semaphore_wait(barrier, len(mates))
+    for step in mates:
+        if step[0]:
+            pl.semaphore_signal(
+                column_in.at[my_row], inc=1, device_id={"ctx": device(step)}, device_id_type=MESH
+            )
+    send(h_out.at[0], h_in.at[0], h_send.at[0], h_recv.at[0], mates)
     place_mixed(0)
-    send_all(x_out.at[0], x_in.at[0], x_send.at[0], x_recv.at[0], own_sem.at[2])
-    send_all(h_out.at[1], h_in.at[1], h_send.at[1], h_recv.at[1], own_sem.at[1])
+    send(e_out, e_in, e_send, e_recv, mates)
+    send(x_out.at[0], x_in.at[0], x_send.at[0], x_recv.at[0], mates)
+    send(h_out.at[1], h_in.at[1], h_send.at[1], h_recv.at[1], mates)
     place_mixed(1)
-    send_all(x_out.at[1], x_in.at[1], x_send.at[1], x_recv.at[1], own_sem.at[3])
+    send(x_out.at[1], x_in.at[1], x_send.at[1], x_recv.at[1], mates)
+    keep(e_out, e_in, own_sem.at[6])
+    for j in range(2):
+        keep(h_out.at[j], h_in.at[j], own_sem.at[j])
+        keep(x_out.at[j], x_in.at[j], own_sem.at[2 + j])
+    for far in (1, side - 1, 2):
+        pl.semaphore_wait(column_in.at[lax.rem(my_row + far, side)], 1)
+        chosen = [step for step in steps if step[0] == far and step[1]]
+        send(h_out.at[0], h_in.at[0], h_send.at[0], h_recv.at[0], chosen)
+        send(e_out, e_in, e_send, e_recv, chosen)
+        send(x_out.at[0], x_in.at[0], x_send.at[0], x_recv.at[0], chosen)
+    chosen = [step for step in steps if step[0] and step[1]]
+    send(h_out.at[1], h_in.at[1], h_send.at[1], h_recv.at[1], chosen)
+    send(x_out.at[1], x_in.at[1], x_send.at[1], x_recv.at[1], chosen)
     loads[4].wait()
     last = proj.at[0, :, pl.ds(width - LANES, LANES)]
     halo = remote(last, q_halo, halo_send, halo_recv, lax.rem(me + 1, n))
@@ -251,26 +288,20 @@
     for load in loads[5:]:
         load.wait()
 
-    for j in range(2):
-        arrived(h_in.at[j], h_recv.at[j], own_sem.at[j])
-        h_freq[...] = forward(h_in[j])
-        if j == 0:
-            arrived(e_in, e_recv, own_sem.at[6], part=whole)
-            place_heads()
-        arrived(x_in.at[j], x_recv.at[j], own_sem.at[2 + j])
-        freq = forward(mixed_of(j))
-        x_re, x_im = freq[:, :SIDE], freq[:, SIDE:]
-        h_re, h_im = h_freq[:, :SIDE], h_freq[:, SIDE:]
-        product = jnp.concatenate(
-            [(x_re * h_re - x_im * h_im).astype(bf16), (x_re * h_im + x_im * h_re).astype(bf16)], axis=1
-        )
-        part = dot(product, bcols[...])
-        real, imag = part[:, :SIDE], part[:, SIDE:]
-        cos, sin = twist[0], twist[1]
-        back[:SIDE] = (real * cos - imag * sin).astype(bf16)
-        back[SIDE:] = (imag * cos + real * sin).astype(bf16)
-        y_out[j] = dot(brows[...], back[...]).astype(bf16)
-        send_all(y_out.at[j], y_in.at[j], y_send.at[j], y_recv.at[j], own_sem.at[4 + j])
+    arrived(h_in.at[0], h_recv.at[0], own_sem.at[0])
+    h_freq[...] = forward([filter_of(0)])
+    arrived(e_in, e_recv, own_sem.at[6])
+    place_heads()
+    arrived(x_in.at[0], x_recv.at[0], own_sem.at[2])
+    y_out[0] = convolved(forward([mixed_of(0)]), h_freq[...])
+    send(y_out.at[0], y_in.at[0], y_send.at[0], y_recv.at[0], steps)
+    keep(y_out.at[0], y_in.at[0], own_sem.at[4])
+    arrived(h_in.at[1], h_recv.at[1], own_sem.at[1])
+    arrived(x_in.at[1], x_recv.at[1], own_sem.at[3])
+    both = forward([mixed_of(1), filter_of(1)])
+    y_out[1] = convolved(both[:SIDE], both[SIDE:])
+    send(y_out.at[1], y_in.at[1], y_send.at[1], y_recv.at[1], steps)
+    keep(y_out.at[1], y_in.at[1], own_sem.at[5])
 
     halo.wait_recv()
     place_gate(0)
@@ -278,8 +309,8 @@
 
     for j in range(2):
         arrived(y_in.at[j], y_recv.at[j], own_sem.at[4 + j])
-        stage[0] = y_in[j, :, 0:LANES].astype(f32)
-        stage[1] = y_in[j, :, LANES:SIDE].astype(f32)
+        stage[0] = y_in[j, :, :, 0:LANES].astype(f32).reshape(SIDE, LANES)
+        stage[1] = y_in[j, :, :, LANES:SIDE].astype(f32).reshape(SIDE, LANES)
 
         def tile_pair(row, carry):
             for parity in range(2):
@@ -306,7 +337,7 @@
     f32, bf16 = jnp.float32, jnp.bfloat16
     outside = pl.BlockSpec(memory_space=pltpu.HBM)
     inside = pl.BlockSpec(memory_space=pltpu.VMEM)
-    square = pltpu.VMEM((2, SIDE, SIDE), bf16)
+    halves = pltpu.VMEM((2, n, SIDE // n, SIDE), bf16)
     edges = pltpu.VMEM((n, 1, LANES), f32)
     pair = pltpu.SemaphoreType.DMA((2,))
     one = pltpu.SemaphoreType.DMA
@@ -329,13 +360,12 @@
             pltpu.VMEM((2, SIDE, LANES), f32),
             pltpu.VMEM((channels, LANES), bf16),
             pltpu.VMEM((2, SIDE, LANES), f32),
-            square, square, square, square, square, square,
-            edges, edges,
+            halves, halves, halves, halves, halves, halves, edges, edges,
             pltpu.VMEM((SIDE, 2 * SIDE), f32),
-            pltpu.VMEM((2 * SIDE, SIDE), bf16),
             pltpu.SemaphoreType.DMA((10,)),
             one, one, pair, pair, pair, pair, pair, pair, one, one,
             pltpu.SemaphoreType.DMA((7,)),
+            pltpu.SemaphoreType.REGULAR((math.isqrt(n),)),
         ],
         compiler_params=pltpu.CompilerParams(
             collective_id=0, has_side_effects=True, vmem_limit_bytes=32 * 1024 * 1024

time: 21.6 us -> 20.6 us (0.954)
  Pallas kernels: 20.8 us -> 19.8 us
    pallas_call x1, Pallas kernels: 20.8 us -> 19.8 us  [shards(): pl.pallas_call(functools.partial(kernel, n), out_shape=jax.ShapeDtypeStru...]
where the time goes in v3:
time: 20.6 us; the launch traced here: 20.5 us
  Pallas kernels  19.8 us (96%)
  local copies, waits for them, and re-layouts  0.71 us (3%)
    pallas_call x1, Pallas kernels, shards(): pl.pallas_call(functools.partial(kernel, n), out_shape=jax.ShapeDtypeStru...  19.8 us
    unnamed x1, local copies, waits for them, and re-layouts  0.71 us

profile of v3, /device:TPU:0, one launch (start us, length us, event | category | flops | bytes accessed | tf_op | source)
XLA Modules:
  0.0 20.5 jit_solution(14260573099105605116)
XLA Ops:
  0.0 19.8 %long_convolution.1 = bf16[32,4096]{1,0:T(8,128)(2,1)S(1)} custom-call(bf16[3,32,4096]{2,1,0:T(8,128)(2,1)} %proj_hbm.1, bf16[32,4096]{1,0:T(8,128)(2,1)} %filt_hbm.1, f32[3,3,32]{2,1,0:T(4,128)} %taps_hbm.1, bf16[512,256]{1,0:T(8,128)(2,1)} %constant.10.clone.rows_hbm, bf16[512,512]{1,0:T(8,128)(2,1)} %constant.11.clone.cols_hbm, ...), custom_call_target="tpu_custom_call" | custom-call | tf_op jit(solution)/shard_map/long_convolution/pallas_call | solution.py:345
  19.8 0.7 %copy.10 = bf16[32,4096]{1,0:T(8,128)(2,1)} copy(bf16[32,4096]{1,0:T(8,128)(2,1)S(1)} %long_convolution.1) | data formatting | bytes 524288

commit v4 on v3

--- a/solution.py
+++ b/solution.py
@@ -14,6 +14,7 @@
 LANES = 128
 SIDE = 256
 TOTAL = SIDE * SIDE
+PARTS = 16
 
 
 def tables():
@@ -24,20 +25,24 @@
         return np.cos(angle), np.sin(angle)
 
     cos, sin = cis(k + 0.25, k, SIDE)
-    rows = np.concatenate([cos, -sin], axis=0)
+    rows = np.concatenate([cos, -sin], axis=1)
     back_rows = np.concatenate([cos.T, -sin.T], axis=1) / TOTAL
     twist = np.stack(cis(k + 0.25, k, TOTAL))
     cos, sin = cis(k, k, SIDE)
     columns = np.block([[cos, -sin], [sin, cos]])
     back_columns = np.block([[cos, sin], [-sin, cos]])
-    bf16 = ml_dtypes.bfloat16
-    return (
-        rows.astype(bf16),
-        columns.astype(bf16),
-        back_columns.astype(bf16),
-        back_rows.astype(bf16),
-        twist.astype(np.float32),
-    )
+    dft = np.concatenate([rows, back_rows, columns, back_columns], axis=0)
+
+    steps = SIDE // PARTS
+    few = np.arange(steps, dtype=np.float64)
+    cos, sin = cis(few + 0.25, few, steps)
+    every = np.eye(PARTS)
+    rows = np.concatenate([np.kron(every, cos), np.kron(every, -sin)], axis=1)
+    back_rows = np.concatenate([np.kron(every, cos.T), np.kron(every, -sin.T)], axis=1) / (steps * SIDE)
+    part_twist = np.stack([np.tile(t, (PARTS, 1)) for t in cis(few + 0.25, k, steps * SIDE)])
+    part_dft = np.concatenate([rows, back_rows], axis=0)
+    bf16, f32 = ml_dtypes.bfloat16, np.float32
+    return dft.astype(bf16), twist.astype(f32), part_dft.astype(bf16), part_twist.astype(f32)
 
 
 def steps_of(n):
@@ -48,11 +53,10 @@
 
 def kernel(
     n,
-    proj_hbm, filt_hbm, taps_hbm, rows_hbm, cols_hbm, bcols_hbm, brows_hbm, twist_hbm,
+    proj_hbm, filt_hbm, taps_hbm, dft_hbm, twist_hbm, part_dft_hbm, part_twist_hbm,
     out,
-    proj, filt, taps_ref, rows, cols, bcols, brows, twist, gate, stage, q_halo, head,
-    h_out, x_out, y_out, h_in, x_in, y_in, e_out, e_in, h_freq,
-    load_sem, halo_send, halo_recv, h_send, h_recv, x_send, x_recv, y_send, y_recv, e_send, e_recv, own_sem, column_in,
+    proj, filt, taps_ref, dft, twist, part_dft, part_twist, gate, stage, q_halo, head, sent, got, e_out, e_in, h_freq,
+    load_sem, halo_send, halo_recv, sent_sem, back_sem, got_sem, e_send, e_recv, column_in,
 ):
     f32, bf16 = jnp.float32, jnp.bfloat16
     me = lax.axis_index("ctx")
@@ -74,13 +78,22 @@
     loads = [
         pltpu.make_async_copy(source, target, load_sem.at[at])
         for at, (source, target) in enumerate([
-            (filt_hbm, filt), (taps_hbm, taps_ref), (proj_hbm.at[1], proj.at[1]), (proj_hbm.at[2], proj.at[2]),
-            (proj_hbm.at[0], proj.at[0]), (rows_hbm, rows), (twist_hbm, twist), (cols_hbm, cols),
-            (bcols_hbm, bcols), (brows_hbm, brows),
+            (filt_hbm, filt), (taps_hbm, taps_ref), (proj_hbm, proj), (dft_hbm, dft), (twist_hbm, twist),
+            (part_dft_hbm, part_dft), (part_twist_hbm, part_twist),
         ])
     ]
-    for load in loads:
+    for load in loads[:5]:
         load.start()
+
+    @pl.when(me == 0)
+    def _():
+        for load in loads[5:]:
+            load.start()
+
+    whole = dft.at[0:SIDE], dft.at[SIDE : 2 * SIDE], twist
+    part = part_dft.at[0:SIDE], part_dft.at[SIDE : 2 * SIDE], part_twist
+    columns, back_columns = dft.at[2 * SIDE : 4 * SIDE], dft.at[4 * SIDE : 6 * SIDE]
+    filters, mixes, results = (0, 2), (1, 3), (4, 5)
 
     def block(ref, at):
         return ref.at[pl.ds(at, 1)]
@@ -91,21 +104,37 @@
             device_id={"ctx": peer}, device_id_type=MESH,
         )
 
-    def send(source, target, send_sem, recv_sem, chosen, part=block):
+    def send(at, chosen):
         for step in chosen:
             peer = device(step)
-            remote(part(source, peer), part(target, me), send_sem, recv_sem, peer).start()
-
-    def keep(source, target, own, part=block):
-        pltpu.make_async_copy(part(source, me), part(target, me), own).start()
+            remote(block(sent.at[at], peer), block(got.at[at], me), sent_sem, got_sem.at[at], peer).start()
+
+    def send_back(at):
+        for step in steps:
+            peer = device(step)
+
+            @pl.when(peer != 0)
+            def _():
+                remote(block(sent.at[at], peer), block(got.at[at], me), back_sem, got_sem.at[at], peer).start()
+
+        @pl.when(me != 0)
+        def _():
+            keep(sent.at[at], got.at[at])
+
+    def send_edges(chosen):
+        for step in chosen:
+            peer = device(step)
+            remote(block(e_out, peer), block(e_in, me), e_send, e_recv, peer).start()
+
+    def keep(source, target):
+        target[pl.ds(me, 1)] = source[pl.ds(me, 1)]
 
     def others(ref, send_sem, recv_sem):
-        size = ref.shape[0] // n * (n - 1)
-        return remote(ref.at[pl.ds(0, size)], ref.at[pl.ds(0, size)], send_sem, recv_sem, me)
-
-    def arrived(target, recv_sem, own, part=block):
-        others(target, recv_sem, recv_sem).wait_recv()
-        pltpu.make_async_copy(part(target, me), part(target, me), own).wait()
+        part = ref.at[pl.ds(0, n - 1)]
+        return remote(part, part, send_sem, recv_sem, me)
+
+    def arrived(at):
+        others(got.at[at], got_sem.at[at], got_sem.at[at]).wait_recv()
 
     def spread(value, group, tile_row, parity):
         stage[parity, pl.ds(group * 8 * 16 + tile_row, 8, stride=16), :] = value
@@ -124,7 +153,8 @@
             return carry
 
         lax.fori_loop(0, tiles // 2, tile_pair, 0, unroll=True)
-        gathered(h_out.at[j])
+        gathered(sent.at[filters[j]])
+        keep(sent.at[filters[j]], got.at[filters[j]])
 
     diagonal = lax.broadcasted_iota(jnp.int32, (half, 2 * half), 0)
     along = lax.broadcasted_iota(jnp.int32, (half, 2 * half), 1)
@@ -169,7 +199,8 @@
             return before
 
         lax.fori_loop(0, tiles // 2, tile_pair, [(zero, zero, zero)] * 2, unroll=True)
-        gathered(x_out.at[j])
+        gathered(sent.at[mixes[j]])
+        keep(sent.at[mixes[j]], got.at[mixes[j]])
 
     def place_edges():
         edges = zero
@@ -182,6 +213,7 @@
                 (lane >= 32 * g + 16) & (lane < 32 * g + 32), pltpu.roll(last, 32 * (g + 1), 1) if g < 3 else last, edges
             )
         e_out[...] = edges[:, None, :]
+        keep(e_out, e_in)
 
     def place_heads():
         edges = e_in[...].reshape(n, LANES)
@@ -203,7 +235,7 @@
         at_row = lax.broadcasted_iota(jnp.int32, (SIDE, LANES), 0)
         at_lane = lax.broadcasted_iota(jnp.int32, (SIDE, LANES), 1)
         is_head = (lax.rem(at_row, 16) == 0) & (at_lane < 2)
-        value = x_in[j].reshape(SIDE, SIDE)
+        value = got[mixes[j]].reshape(SIDE, SIDE)
         even = jnp.where(is_head, head[j], value[:, 0:LANES].astype(f32)).astype(bf16)
         return jnp.concatenate([even, value[:, LANES:SIDE]], axis=1)
 
@@ -221,96 +253,103 @@
     def dot(a, b):
         return jnp.dot(a, b, preferred_element_type=f32)
 
-    def forward(values):
-        part = dot(rows[...], jnp.concatenate(values, axis=1))
+    def forward(values, of):
+        rows, _, twist = of
+        values = jnp.concatenate(values, axis=1)
+        reals, imags = dot(rows[:, :SIDE], values), dot(rows[:, SIDE:], values)
         cos, sin = twist[0], twist[1]
         turned = []
-        for at in range(len(values)):
-            columns = slice(SIDE * at, SIDE * (at + 1))
-            real, imag = part[:SIDE, columns], part[SIDE:, columns]
+        for at in range(values.shape[1] // SIDE):
+            own = slice(SIDE * at, SIDE * (at + 1))
+            real, imag = reals[:, own], imags[:, own]
             turned.append(
                 jnp.concatenate([(real * cos + imag * sin).astype(bf16), (imag * cos - real * sin).astype(bf16)], axis=1)
             )
-        return dot(jnp.concatenate(turned, axis=0), cols[...])
-
-    def convolved(x, h):
+        return dot(jnp.concatenate(turned, axis=0), columns[...])
+
+    def convolved(x, h, of):
+        _, back_rows, twist = of
         x_re, x_im, h_re, h_im = x[:, :SIDE], x[:, SIDE:], h[:, :SIDE], h[:, SIDE:]
         product = jnp.concatenate(
             [(x_re * h_re - x_im * h_im).astype(bf16), (x_re * h_im + x_im * h_re).astype(bf16)], axis=1
         )
-        part = dot(product, bcols[...])
-        real, imag = part[:, :SIDE], part[:, SIDE:]
+        values = dot(product, back_columns[...])
+        real, imag = values[:, :SIDE], values[:, SIDE:]
         cos, sin = twist[0], twist[1]
         turned = jnp.concatenate(
             [(real * cos - imag * sin).astype(bf16), (imag * cos + real * sin).astype(bf16)], axis=0
         )
-        return dot(brows[...], turned).astype(bf16).reshape(n, 16, SIDE)
+        return dot(back_rows[...], turned).astype(bf16).reshape(n, 16, SIDE)
 
     def filter_of(j):
-        return h_in[j].reshape(SIDE, SIDE)
+        return got[filters[j]].reshape(SIDE, SIDE)
 
     loads[0].wait()
     place_filter(0)
     place_filter(1)
-    for load in loads[1:4]:
-        load.wait()
+    loads[1].wait()
+    loads[2].wait()
     place_edges()
     pl.semaphore_wait(barrier, len(mates))
     for step in mates:
         if step[0]:
             pl.semaphore_signal(
-                column_in.at[my_row], inc=1, device_id={"ctx": device(step)}, device_id_type=MESH
+                column_in.at[side - 1 - step[0]], inc=1, device_id={"ctx": device(step)}, device_id_type=MESH
             )
-    send(h_out.at[0], h_in.at[0], h_send.at[0], h_recv.at[0], mates)
+    send(filters[0], mates)
     place_mixed(0)
-    send(e_out, e_in, e_send, e_recv, mates)
-    send(x_out.at[0], x_in.at[0], x_send.at[0], x_recv.at[0], mates)
-    send(h_out.at[1], h_in.at[1], h_send.at[1], h_recv.at[1], mates)
+    send_edges(mates)
+    send(mixes[0], mates)
+    send(filters[1], mates)
     place_mixed(1)
-    send(x_out.at[1], x_in.at[1], x_send.at[1], x_recv.at[1], mates)
-    keep(e_out, e_in, own_sem.at[6])
-    for j in range(2):
-        keep(h_out.at[j], h_in.at[j], own_sem.at[j])
-        keep(x_out.at[j], x_in.at[j], own_sem.at[2 + j])
+    send(mixes[1], mates)
     for far in (1, side - 1, 2):
-        pl.semaphore_wait(column_in.at[lax.rem(my_row + far, side)], 1)
+        pl.semaphore_wait(column_in.at[far - 1], 1)
         chosen = [step for step in steps if step[0] == far and step[1]]
-        send(h_out.at[0], h_in.at[0], h_send.at[0], h_recv.at[0], chosen)
-        send(e_out, e_in, e_send, e_recv, chosen)
-        send(x_out.at[0], x_in.at[0], x_send.at[0], x_recv.at[0], chosen)
+        send(filters[0], chosen)
+        send_edges(chosen)
+        send(mixes[0], chosen)
     chosen = [step for step in steps if step[0] and step[1]]
-    send(h_out.at[1], h_in.at[1], h_send.at[1], h_recv.at[1], chosen)
-    send(x_out.at[1], x_in.at[1], x_send.at[1], x_recv.at[1], chosen)
-    loads[4].wait()
+    send(filters[1], chosen)
+    send(mixes[1], chosen)
     last = proj.at[0, :, pl.ds(width - LANES, LANES)]
     halo = remote(last, q_halo, halo_send, halo_recv, lax.rem(me + 1, n))
     halo.start()
-    for load in loads[5:]:
+    for load in loads[3:5]:
         load.wait()
 
-    arrived(h_in.at[0], h_recv.at[0], own_sem.at[0])
-    h_freq[...] = forward([filter_of(0)])
-    arrived(e_in, e_recv, own_sem.at[6])
+    @pl.when(me == 0)
+    def _():
+        for load in loads[5:]:
+            load.wait()
+        for j in range(2):
+            both = forward([sent[at[j]].reshape(SIDE, SIDE) for at in (mixes, filters)], part)
+            got[results[j]] = convolved(both[:SIDE], both[SIDE:], part)
+
+    arrived(filters[0])
+    h_freq[...] = forward([filter_of(0)], whole)
+    others(e_in, e_recv, e_recv).wait_recv()
     place_heads()
-    arrived(x_in.at[0], x_recv.at[0], own_sem.at[2])
-    y_out[0] = convolved(forward([mixed_of(0)]), h_freq[...])
-    send(y_out.at[0], y_in.at[0], y_send.at[0], y_recv.at[0], steps)
-    keep(y_out.at[0], y_in.at[0], own_sem.at[4])
-    arrived(h_in.at[1], h_recv.at[1], own_sem.at[1])
-    arrived(x_in.at[1], x_recv.at[1], own_sem.at[3])
-    both = forward([mixed_of(1), filter_of(1)])
-    y_out[1] = convolved(both[:SIDE], both[SIDE:])
-    send(y_out.at[1], y_in.at[1], y_send.at[1], y_recv.at[1], steps)
-    keep(y_out.at[1], y_in.at[1], own_sem.at[5])
+    arrived(mixes[0])
+    sent[results[0]] = convolved(forward([mixed_of(0)], whole), h_freq[...], whole)
+    send_back(results[0])
+    arrived(filters[1])
+    arrived(mixes[1])
+    both = forward([mixed_of(1), filter_of(1)], whole)
+    sent[results[1]] = convolved(both[:SIDE], both[SIDE:], whole)
+    send_back(results[1])
 
     halo.wait_recv()
     place_gate(0)
     place_gate(1)
 
     for j in range(2):
-        arrived(y_in.at[j], y_recv.at[j], own_sem.at[4 + j])
-        stage[0] = y_in[j, :, :, 0:LANES].astype(f32).reshape(SIDE, LANES)
-        stage[1] = y_in[j, :, :, LANES:SIDE].astype(f32).reshape(SIDE, LANES)
+        @pl.when(me != 0)
+        def _():
+            arrived(results[j])
+
+        stage[0] = got[results[j], :, :, 0:LANES].astype(f32).reshape(SIDE, LANES)
+        stage[1] = got[results[j], :, :, LANES:SIDE].astype(f32).reshape(SIDE, LANES)
 
         def tile_pair(row, carry):
             for parity in range(2):
@@ -326,10 +365,19 @@
 
     halo.wait_send()
     others(e_out, e_send, e_send).wait_send()
-    for j in range(2):
-        others(h_out.at[j], h_send.at[j], h_send.at[j]).wait_send()
-        others(x_out.at[j], x_send.at[j], x_send.at[j]).wait_send()
-        others(y_out.at[j], y_send.at[j], y_send.at[j]).wait_send()
+
+    def all_sent(ref, sem):
+        remote(ref, ref, sem, sem, me).wait_send()
+
+    all_sent(sent.at[0:4, 0 : n - 1], sent_sem)
+
+    @pl.when(me == 0)
+    def _():
+        all_sent(sent.at[4:6, 0 : n - 1], back_sem)
+
+    @pl.when(me != 0)
+    def _():
+        all_sent(sent.at[4:6, 0 : n - 2], back_sem)
 
 
 def shards(n, projections, short_taps, long_filter):
@@ -337,35 +385,34 @@
     f32, bf16 = jnp.float32, jnp.bfloat16
     outside = pl.BlockSpec(memory_space=pltpu.HBM)
     inside = pl.BlockSpec(memory_space=pltpu.VMEM)
-    halves = pltpu.VMEM((2, n, SIDE // n, SIDE), bf16)
     edges = pltpu.VMEM((n, 1, LANES), f32)
-    pair = pltpu.SemaphoreType.DMA((2,))
+    parts = pltpu.VMEM((6, n, SIDE // n, SIDE), bf16)
     one = pltpu.SemaphoreType.DMA
     operands = [projections, long_filter, short_taps, *(jnp.asarray(t) for t in tables())]
     return pl.pallas_call(
         functools.partial(kernel, n),
         out_shape=jax.ShapeDtypeStruct((channels, width), bf16),
-        in_specs=[outside] * 8,
+        in_specs=[outside] * len(operands),
         out_specs=inside,
         scratch_shapes=[
             pltpu.VMEM((3, channels, width), bf16),
             pltpu.VMEM((channels, width), bf16),
             pltpu.VMEM((3, 3, channels), f32),
-            pltpu.VMEM((2 * SIDE, SIDE), bf16),
+            pltpu.VMEM((6 * SIDE, 2 * SIDE), bf16),
+            pltpu.VMEM((2, SIDE, SIDE), f32),
             pltpu.VMEM((2 * SIDE, 2 * SIDE), bf16),
-            pltpu.VMEM((2 * SIDE, 2 * SIDE), bf16),
-            pltpu.VMEM((SIDE, 2 * SIDE), bf16),
             pltpu.VMEM((2, SIDE, SIDE), f32),
             pltpu.VMEM((channels, width), f32),
             pltpu.VMEM((2, SIDE, LANES), f32),
             pltpu.VMEM((channels, LANES), bf16),
             pltpu.VMEM((2, SIDE, LANES), f32),
-            halves, halves, halves, halves, halves, halves, edges, edges,
+            parts, parts, edges, edges,
             pltpu.VMEM((SIDE, 2 * SIDE), f32),
-            pltpu.SemaphoreType.DMA((10,)),
-            one, one, pair, pair, pair, pair, pair, pair, one, one,
-            pltpu.SemaphoreType.DMA((7,)),
-            pltpu.SemaphoreType.REGULAR((math.isqrt(n),)),
+            pltpu.SemaphoreType.DMA((len(operands),)),
+            one, one, one, one,
+            pltpu.SemaphoreType.DMA((6,)),
+            one, one,
+            pltpu.SemaphoreType.REGULAR((math.isqrt(n) - 1,)),
         ],
         compiler_params=pltpu.CompilerParams(
             collective_id=0, has_side_effects=True, vmem_limit_bytes=32 * 1024 * 1024

time: 20.6 us -> 19.6 us (0.951)
  the two profiles are of different devices: /device:TPU:0 before, /device:TPU:66 now
where the time goes in v4:
time: 19.6 us; the launch traced here: 19.5 us
  Pallas kernels  18.8 us (96%)
  local copies, waits for them, and re-layouts  0.71 us (4%)
    pallas_call x1, Pallas kernels, shards(): pl.pallas_call(functools.partial(kernel, n), out_shape=jax.ShapeDtypeStru...  18.8 us
    unnamed x1, local copies, waits for them, and re-layouts  0.71 us

profile of v4, /device:TPU:66, one launch (start us, length us, event | category | flops | bytes accessed | tf_op | source)
XLA Modules:
  0.0 19.5 jit_solution(15780983375833725035)
XLA Ops:
  0.0 18.8 %long_convolution.1 = bf16[32,4096]{1,0:T(8,128)(2,1)S(1)} custom-call(bf16[3,32,4096]{2,1,0:T(8,128)(2,1)} %proj_hbm.1, bf16[32,4096]{1,0:T(8,128)(2,1)} %filt_hbm.1, f32[3,3,32]{2,1,0:T(4,128)} %taps_hbm.1, bf16[1536,512]{1,0:T(8,128)(2,1)} %constant.8.clone.dft_hbm, f32[2,256,256]{2,1,0:T(8,128)} %constant.9.clone.twist_hbm, ...), custom_call_target="tpu_custom_call" | custom-call | tf_op jit(solution)/shard_map/long_convolution/pallas_call | solution.py:392
  18.8 0.7 %copy.9 = bf16[32,4096]{1,0:T(8,128)(2,1)} copy(bf16[32,4096]{1,0:T(8,128)(2,1)S(1)} %long_convolution.1) | data formatting | bytes 524288

commit v5 on v4

--- a/solution.py
+++ b/solution.py
@@ -31,7 +31,7 @@
     cos, sin = cis(k, k, SIDE)
     columns = np.block([[cos, -sin], [sin, cos]])
     back_columns = np.block([[cos, sin], [-sin, cos]])
-    dft = np.concatenate([rows, back_rows, columns, back_columns], axis=0)
+    dft = [rows, back_rows, columns, back_columns]
 
     steps = SIDE // PARTS
     few = np.arange(steps, dtype=np.float64)
@@ -40,9 +40,8 @@
     rows = np.concatenate([np.kron(every, cos), np.kron(every, -sin)], axis=1)
     back_rows = np.concatenate([np.kron(every, cos.T), np.kron(every, -sin.T)], axis=1) / (steps * SIDE)
     part_twist = np.stack([np.tile(t, (PARTS, 1)) for t in cis(few + 0.25, k, steps * SIDE)])
-    part_dft = np.concatenate([rows, back_rows], axis=0)
-    bf16, f32 = ml_dtypes.bfloat16, np.float32
-    return dft.astype(bf16), twist.astype(f32), part_dft.astype(bf16), part_twist.astype(f32)
+    dft = np.concatenate(dft + [rows, back_rows], axis=0)
+    return dft.astype(ml_dtypes.bfloat16), np.concatenate([twist, part_twist]).astype(np.float32)
 
 
 def steps_of(n):
@@ -53,9 +52,9 @@
 
 def kernel(
     n,
-    proj_hbm, filt_hbm, taps_hbm, dft_hbm, twist_hbm, part_dft_hbm, part_twist_hbm,
+    proj_hbm, filt_hbm, taps_hbm, dft_hbm, twist_hbm,
     out,
-    proj, filt, taps_ref, dft, twist, part_dft, part_twist, gate, stage, q_halo, head, sent, got, e_out, e_in, h_freq,
+    proj, filt, taps_ref, dft, twists, gate, stage, q_halo, head, sent, got, e_out, e_in, h_freq,
     load_sem, halo_send, halo_recv, sent_sem, back_sem, got_sem, e_send, e_recv, column_in,
 ):
     f32, bf16 = jnp.float32, jnp.bfloat16
@@ -78,20 +77,13 @@
     loads = [
         pltpu.make_async_copy(source, target, load_sem.at[at])
         for at, (source, target) in enumerate([
-            (filt_hbm, filt), (taps_hbm, taps_ref), (proj_hbm, proj), (dft_hbm, dft), (twist_hbm, twist),
-            (part_dft_hbm, part_dft), (part_twist_hbm, part_twist),
+            (filt_hbm, filt), (taps_hbm, taps_ref), (proj_hbm, proj), (dft_hbm, dft), (twist_hbm, twists),
         ])
     ]
-    for load in loads[:5]:
+    for load in loads:
         load.start()
-
-    @pl.when(me == 0)
-    def _():
-        for load in loads[5:]:
-            load.start()
-
-    whole = dft.at[0:SIDE], dft.at[SIDE : 2 * SIDE], twist
-    part = part_dft.at[0:SIDE], part_dft.at[SIDE : 2 * SIDE], part_twist
+    whole = dft.at[0:SIDE], dft.at[SIDE : 2 * SIDE], twists.at[0:2]
+    part = dft.at[6 * SIDE : 7 * SIDE], dft.at[7 * SIDE : 8 * SIDE], twists.at[2:4]
     columns, back_columns = dft.at[2 * SIDE : 4 * SIDE], dft.at[4 * SIDE : 6 * SIDE]
     filters, mixes, results = (0, 2), (1, 3), (4, 5)
 
@@ -107,7 +99,7 @@
     def send(at, chosen):
         for step in chosen:
             peer = device(step)
-            remote(block(sent.at[at], peer), block(got.at[at], me), sent_sem, got_sem.at[at], peer).start()
+            remote(block(sent.at[at], peer), block(got.at[at], me), sent_sem, got_sem.at[min(at, 2)], peer).start()
 
     def send_back(at):
         for step in steps:
@@ -115,7 +107,7 @@
 
             @pl.when(peer != 0)
             def _():
-                remote(block(sent.at[at], peer), block(got.at[at], me), back_sem, got_sem.at[at], peer).start()
+                remote(block(sent.at[at], peer), block(got.at[at], me), back_sem, got_sem.at[at - 1], peer).start()
 
         @pl.when(me != 0)
         def _():
@@ -133,8 +125,8 @@
         part = ref.at[pl.ds(0, n - 1)]
         return remote(part, part, send_sem, recv_sem, me)
 
-    def arrived(at):
-        others(got.at[at], got_sem.at[at], got_sem.at[at]).wait_recv()
+    def arrived(at, sem):
+        others(got.at[at], got_sem.at[sem], got_sem.at[sem]).wait_recv()
 
     def spread(value, group, tile_row, parity):
         stage[parity, pl.ds(group * 8 * 16 + tile_row, 8, stride=16), :] = value
@@ -296,45 +288,45 @@
             pl.semaphore_signal(
                 column_in.at[side - 1 - step[0]], inc=1, device_id={"ctx": device(step)}, device_id_type=MESH
             )
+    send_edges(mates)
     send(filters[0], mates)
     place_mixed(0)
-    send_edges(mates)
     send(mixes[0], mates)
-    send(filters[1], mates)
+    send(filters[1], [step for step in mates if 2 not in step])
     place_mixed(1)
-    send(mixes[1], mates)
+    send(mixes[1], [step for step in mates if 2 not in step])
     for far in (1, side - 1, 2):
         pl.semaphore_wait(column_in.at[far - 1], 1)
         chosen = [step for step in steps if step[0] == far and step[1]]
+        send_edges(chosen)
         send(filters[0], chosen)
-        send_edges(chosen)
         send(mixes[0], chosen)
     chosen = [step for step in steps if step[0] and step[1]]
     send(filters[1], chosen)
     send(mixes[1], chosen)
+    send(filters[1], [step for step in mates if 2 in step])
+    send(mixes[1], [step for step in mates if 2 in step])
     last = proj.at[0, :, pl.ds(width - LANES, LANES)]
     halo = remote(last, q_halo, halo_send, halo_recv, lax.rem(me + 1, n))
     halo.start()
-    for load in loads[3:5]:
+    for load in loads[3:]:
         load.wait()
 
     @pl.when(me == 0)
     def _():
-        for load in loads[5:]:
-            load.wait()
         for j in range(2):
             both = forward([sent[at[j]].reshape(SIDE, SIDE) for at in (mixes, filters)], part)
             got[results[j]] = convolved(both[:SIDE], both[SIDE:], part)
 
-    arrived(filters[0])
+    others(e_in, e_recv, e_recv).wait_recv()
+    arrived(filters[0], 0)
+    place_heads()
     h_freq[...] = forward([filter_of(0)], whole)
-    others(e_in, e_recv, e_recv).wait_recv()
-    place_heads()
-    arrived(mixes[0])
+    arrived(mixes[0], 1)
     sent[results[0]] = convolved(forward([mixed_of(0)], whole), h_freq[...], whole)
     send_back(results[0])
-    arrived(filters[1])
-    arrived(mixes[1])
+    pair = got.at[filters[1] : mixes[1] + 1, 0 : n - 1]
+    remote(pair, pair, got_sem.at[2], got_sem.at[2], me).wait_recv()
     both = forward([mixed_of(1), filter_of(1)], whole)
     sent[results[1]] = convolved(both[:SIDE], both[SIDE:], whole)
     send_back(results[1])
@@ -346,7 +338,7 @@
     for j in range(2):
         @pl.when(me != 0)
         def _():
-            arrived(results[j])
+            arrived(results[j], 3 + j)
 
         stage[0] = got[results[j], :, :, 0:LANES].astype(f32).reshape(SIDE, LANES)
         stage[1] = got[results[j], :, :, LANES:SIDE].astype(f32).reshape(SIDE, LANES)
@@ -398,10 +390,8 @@
             pltpu.VMEM((3, channels, width), bf16),
             pltpu.VMEM((channels, width), bf16),
             pltpu.VMEM((3, 3, channels), f32),
-            pltpu.VMEM((6 * SIDE, 2 * SIDE), bf16),
-            pltpu.VMEM((2, SIDE, SIDE), f32),
-            pltpu.VMEM((2 * SIDE, 2 * SIDE), bf16),
-            pltpu.VMEM((2, SIDE, SIDE), f32),
+            pltpu.VMEM((8 * SIDE, 2 * SIDE), bf16),
+            pltpu.VMEM((4, SIDE, SIDE), f32),
             pltpu.VMEM((channels, width), f32),
             pltpu.VMEM((2, SIDE, LANES), f32),
             pltpu.VMEM((channels, LANES), bf16),
@@ -410,7 +400,7 @@
             pltpu.VMEM((SIDE, 2 * SIDE), f32),
             pltpu.SemaphoreType.DMA((len(operands),)),
             one, one, one, one,
-            pltpu.SemaphoreType.DMA((6,)),
+            pltpu.SemaphoreType.DMA((5,)),
             one, one,
             pltpu.SemaphoreType.REGULAR((math.isqrt(n) - 1,)),
         ],

time: 19.6 us -> 19.4 us (0.990)
  Pallas kernels: 18.8 us -> 18.6 us
    pallas_call x1, Pallas kernels: 18.8 us -> 18.6 us  [shards(): pl.pallas_call(functools.partial(kernel, n), out_shape=jax.ShapeDtypeStru...]
where the time goes in v5:
time: 19.4 us; the launch traced here: 19.3 us
  Pallas kernels  18.6 us (96%)
  local copies, waits for them, and re-layouts  0.71 us (4%)
    pallas_call x1, Pallas kernels, shards(): pl.pallas_call(functools.partial(kernel, n), out_shape=jax.ShapeDtypeStru...  18.6 us
    unnamed x1, local copies, waits for them, and re-layouts  0.71 us

profile of v5, /device:TPU:66, one launch (start us, length us, event | category | flops | bytes accessed | tf_op | source)
XLA Modules:
  0.0 19.3 jit_solution(9209363286775088259)
XLA Ops:
  0.0 18.6 %long_convolution.1 = bf16[32,4096]{1,0:T(8,128)(2,1)S(1)} custom-call(bf16[3,32,4096]{2,1,0:T(8,128)(2,1)} %proj_hbm.1, bf16[32,4096]{1,0:T(8,128)(2,1)} %filt_hbm.1, f32[3,3,32]{2,1,0:T(4,128)} %taps_hbm.1, bf16[2048,512]{1,0:T(8,128)(2,1)} %constant.4.clone.dft_hbm, f32[4,256,256]{2,1,0:T(8,128)} %constant.5.clone.twist_hbm), custom_call_target="tpu_custom_call" | custom-call | tf_op jit(solution)/shard_map/long_convolution/pallas_call | solution.py:384
  18.6 0.7 %copy.7 = bf16[32,4096]{1,0:T(8,128)(2,1)} copy(bf16[32,4096]{1,0:T(8,128)(2,1)S(1)} %long_convolution.1) | data formatting | bytes 524288

commit v6 on v5

--- a/solution.py
+++ b/solution.py
@@ -80,7 +80,7 @@
             (filt_hbm, filt), (taps_hbm, taps_ref), (proj_hbm, proj), (dft_hbm, dft), (twist_hbm, twists),
         ])
     ]
-    for load in loads:
+    for load in loads[:3]:
         load.start()
     whole = dft.at[0:SIDE], dft.at[SIDE : 2 * SIDE], twists.at[0:2]
     part = dft.at[6 * SIDE : 7 * SIDE], dft.at[7 * SIDE : 8 * SIDE], twists.at[2:4]
@@ -281,6 +281,8 @@
     place_filter(1)
     loads[1].wait()
     loads[2].wait()
+    for load in loads[3:]:
+        load.start()
     place_edges()
     pl.semaphore_wait(barrier, len(mates))
     for step in mates:

time: 19.4 us -> 19.4 us (level)
  no operation moved by 1% of the time
where the time goes in v6:
time: 19.4 us; the launch traced here: 19.3 us
  Pallas kernels  18.6 us (96%)
  local copies, waits for them, and re-layouts  0.71 us (4%)
    pallas_call x1, Pallas kernels, shards(): pl.pallas_call(functools.partial(kernel, n), out_shape=jax.ShapeDtypeStru...  18.6 us
    unnamed x1, local copies, waits for them, and re-layouts  0.71 us

profile of v6, /device:TPU:66, one launch (start us, length us, event | category | flops | bytes accessed | tf_op | source)
XLA Modules:
  0.0 19.3 jit_solution(5159460528386234333)
XLA Ops:
  0.0 18.6 %long_convolution.1 = bf16[32,4096]{1,0:T(8,128)(2,1)S(1)} custom-call(bf16[3,32,4096]{2,1,0:T(8,128)(2,1)} %proj_hbm.1, bf16[32,4096]{1,0:T(8,128)(2,1)} %filt_hbm.1, f32[3,3,32]{2,1,0:T(4,128)} %taps_hbm.1, bf16[2048,512]{1,0:T(8,128)(2,1)} %constant.4.clone.dft_hbm, f32[4,256,256]{2,1,0:T(8,128)} %constant.5.clone.twist_hbm), custom_call_target="tpu_custom_call" | custom-call | tf_op jit(solution)/shard_map/long_convolution/pallas_call | solution.py:386
  18.6 0.7 %copy.7 = bf16[32,4096]{1,0:T(8,128)(2,1)} copy(bf16[32,4096]{1,0:T(8,128)(2,1)S(1)} %long_convolution.1) | data formatting | bytes 524288

commit v7 on v5

--- a/solution.py
+++ b/solution.py
@@ -55,7 +55,7 @@
     proj_hbm, filt_hbm, taps_hbm, dft_hbm, twist_hbm,
     out,
     proj, filt, taps_ref, dft, twists, gate, stage, q_halo, head, sent, got, e_out, e_in, h_freq,
-    load_sem, halo_send, halo_recv, sent_sem, back_sem, got_sem, e_send, e_recv, column_in,
+    load_sem, halo_recv, sent_sem, got_sem, e_recv, column_in,
 ):
     f32, bf16 = jnp.float32, jnp.bfloat16
     me = lax.axis_index("ctx")
@@ -107,7 +107,7 @@
 
             @pl.when(peer != 0)
             def _():
-                remote(block(sent.at[at], peer), block(got.at[at], me), back_sem, got_sem.at[at - 1], peer).start()
+                remote(block(sent.at[at], peer), block(got.at[at], me), sent_sem, got_sem.at[at - 1], peer).start()
 
         @pl.when(me != 0)
         def _():
@@ -116,7 +116,7 @@
     def send_edges(chosen):
         for step in chosen:
             peer = device(step)
-            remote(block(e_out, peer), block(e_in, me), e_send, e_recv, peer).start()
+            remote(block(e_out, peer), block(e_in, me), sent_sem, e_recv, peer).start()
 
     def keep(source, target):
         target[pl.ds(me, 1)] = source[pl.ds(me, 1)]
@@ -307,7 +307,7 @@
     send(filters[1], [step for step in mates if 2 in step])
     send(mixes[1], [step for step in mates if 2 in step])
     last = proj.at[0, :, pl.ds(width - LANES, LANES)]
-    halo = remote(last, q_halo, halo_send, halo_recv, lax.rem(me + 1, n))
+    halo = remote(last, q_halo, sent_sem, halo_recv, lax.rem(me + 1, n))
     halo.start()
     for load in loads[3:]:
         load.wait()
@@ -356,7 +356,7 @@
         lax.fori_loop(0, tiles // 2, tile_pair, 0, unroll=True)
 
     halo.wait_send()
-    others(e_out, e_send, e_send).wait_send()
+    others(e_out, sent_sem, sent_sem).wait_send()
 
     def all_sent(ref, sem):
         remote(ref, ref, sem, sem, me).wait_send()
@@ -365,11 +365,11 @@
 
     @pl.when(me == 0)
     def _():
-        all_sent(sent.at[4:6, 0 : n - 1], back_sem)
+        all_sent(sent.at[4:6, 0 : n - 1], sent_sem)
 
     @pl.when(me != 0)
     def _():
-        all_sent(sent.at[4:6, 0 : n - 2], back_sem)
+        all_sent(sent.at[4:6, 0 : n - 2], sent_sem)
 
 
 def shards(n, projections, short_taps, long_filter):
@@ -399,9 +399,9 @@
             parts, parts, edges, edges,
             pltpu.VMEM((SIDE, 2 * SIDE), f32),
             pltpu.SemaphoreType.DMA((len(operands),)),
-            one, one, one, one,
+            one, one,
             pltpu.SemaphoreType.DMA((5,)),
-            one, one,
+            one,
             pltpu.SemaphoreType.REGULAR((math.isqrt(n) - 1,)),
         ],
         compiler_params=pltpu.CompilerParams(

time: 19.4 us -> 19.4 us (level)
  no operation moved by 1% of the time
where the time goes in v7:
time: 19.4 us; the launch traced here: 19.3 us
  Pallas kernels  18.5 us (95%)
  local copies, waits for them, and re-layouts  0.71 us (4%)
    pallas_call x1, Pallas kernels, shards(): pl.pallas_call(functools.partial(kernel, n), out_shape=jax.ShapeDtypeStru...  18.5 us
    unnamed x1, local copies, waits for them, and re-layouts  0.71 us

profile of v7, /device:TPU:66, one launch (start us, length us, event | category | flops | bytes accessed | tf_op | source)
XLA Modules:
  0.0 19.3 jit_solution(14873091862067470242)
XLA Ops:
  0.0 18.5 %long_convolution.1 = bf16[32,4096]{1,0:T(8,128)(2,1)S(1)} custom-call(bf16[3,32,4096]{2,1,0:T(8,128)(2,1)} %proj_hbm.1, bf16[32,4096]{1,0:T(8,128)(2,1)} %filt_hbm.1, f32[3,3,32]{2,1,0:T(4,128)} %taps_hbm.1, bf16[2048,512]{1,0:T(8,128)(2,1)} %constant.4.clone.dft_hbm, f32[4,256,256]{2,1,0:T(8,128)} %constant.5.clone.twist_hbm), custom_call_target="tpu_custom_call" | custom-call | tf_op jit(solution)/shard_map/long_convolution/pallas_call | solution.py:384
  18.5 0.7 %copy.7 = bf16[32,4096]{1,0:T(8,128)(2,1)} copy(bf16[32,4096]{1,0:T(8,128)(2,1)S(1)} %long_convolution.1) | data formatting | bytes 524288

commit v8 on v5

--- a/solution.py
+++ b/solution.py
@@ -66,6 +66,8 @@
         return lax.rem(my_row + step[0], side) * side + lax.rem(my_column + step[1], side)
 
     steps = steps_of(n)
+    beside = [step for step in steps if sum(step) in (1, side - 1) and 0 in step]
+    beyond = [step for step in steps if step not in beside]
     mates = [step for step in steps if not (step[0] and step[1])]
     width = filt.shape[1]
     tiles = width // LANES
@@ -101,17 +103,13 @@
             peer = device(step)
             remote(block(sent.at[at], peer), block(got.at[at], me), sent_sem, got_sem.at[min(at, 2)], peer).start()
 
-    def send_back(at):
-        for step in steps:
+    def send_back(at, chosen):
+        for step in chosen:
             peer = device(step)
 
             @pl.when(peer != 0)
             def _():
                 remote(block(sent.at[at], peer), block(got.at[at], me), back_sem, got_sem.at[at - 1], peer).start()
-
-        @pl.when(me != 0)
-        def _():
-            keep(sent.at[at], got.at[at])
 
     def send_edges(chosen):
         for step in chosen:
@@ -324,12 +322,23 @@
     h_freq[...] = forward([filter_of(0)], whole)
     arrived(mixes[0], 1)
     sent[results[0]] = convolved(forward([mixed_of(0)], whole), h_freq[...], whole)
-    send_back(results[0])
+    send_back(results[0], beyond)
+
+    @pl.when(me != 0)
+    def _():
+        keep(sent.at[results[0]], got.at[results[0]])
+
     pair = got.at[filters[1] : mixes[1] + 1, 0 : n - 1]
     remote(pair, pair, got_sem.at[2], got_sem.at[2], me).wait_recv()
+    send_back(results[0], beside)
     both = forward([mixed_of(1), filter_of(1)], whole)
     sent[results[1]] = convolved(both[:SIDE], both[SIDE:], whole)
-    send_back(results[1])
+    send_back(results[1], steps)
+
+    @pl.when(me != 0)
+    def _():
+        keep(sent.at[results[1]], got.at[results[1]])
+
 
     halo.wait_recv()
     place_gate(0)

time: 19.4 us -> 19.4 us (level)
  no operation moved by 1% of the time
where the time goes in v8:
time: 19.4 us; the launch traced here: 19.3 us
  Pallas kernels  18.6 us (96%)
  local copies, waits for them, and re-layouts  0.71 us (4%)
    pallas_call x1, Pallas kernels, shards(): pl.pallas_call(functools.partial(kernel, n), out_shape=jax.ShapeDtypeStru...  18.6 us
    unnamed x1, local copies, waits for them, and re-layouts  0.71 us

profile of v8, /device:TPU:66, one launch (start us, length us, event | category | flops | bytes accessed | tf_op | source)
XLA Modules:
  0.0 19.3 jit_solution(8818523938886843060)
XLA Ops:
  0.0 18.6 %long_convolution.1 = bf16[32,4096]{1,0:T(8,128)(2,1)S(1)} custom-call(bf16[3,32,4096]{2,1,0:T(8,128)(2,1)} %proj_hbm.1, bf16[32,4096]{1,0:T(8,128)(2,1)} %filt_hbm.1, f32[3,3,32]{2,1,0:T(4,128)} %taps_hbm.1, bf16[2048,512]{1,0:T(8,128)(2,1)} %constant.4.clone.dft_hbm, f32[4,256,256]{2,1,0:T(8,128)} %constant.5.clone.twist_hbm), custom_call_target="tpu_custom_call" | custom-call | tf_op jit(solution)/shard_map/long_convolution/pallas_call | solution.py:393
  18.6 0.7 %copy.7 = bf16[32,4096]{1,0:T(8,128)(2,1)} copy(bf16[32,4096]{1,0:T(8,128)(2,1)S(1)} %long_convolution.1) | data formatting | bytes 524288
